TPU v7x, 512 devices: a whole 4x8x8 slice. The times are simulated.
512 devices in a mesh: rep: 64 (over z, y), slab: 8 (over x, core).
Axes of the slice: x: 4, y: 8, z: 8, core: 2. Of those that a mesh axis runs over, the one named last changes fastest.
Arguments:
- features: bfloat16 [64, 24, 32, 8, 128], P('rep', None, 'slab'), may hold values from -6 to 6
- cotangent: bfloat16 [64, 16, 32, 8, 128], P('rep', None, 'slab'), may hold values from -6 to 6
- conv_weight: bfloat16 [24, 24, 3, 3, 3], replicated, may hold values from -0.25 to 0.25
- conv_bias: float32 [24], replicated, may hold values from -3 to 3
- head_weight: bfloat16 [24, 16], replicated, may hold values from -1.25 to 1.25
- grad_rest: float32 [64, 8, 246168], P('rep', 'slab'), may hold values from -6400 to 6400
- master: float32 [262144], P('rep'), may hold values from -1.2 to 1.2
- moment: float32 [262144], P('rep'), may hold values from -6 to 6
- second: float32 [262144], P('rep'), may hold values from 0.5 to 4
Outputs:
- input_grad: bfloat16 [64, 24, 32, 8, 128], P('rep', None, 'slab')
- new_moment: float32 [262144], P('rep')
- new_second: float32 [262144], P('rep')
- new_master: float32 [262144], P('rep')
- weights: bfloat16 [262144], replicated
All inputs are finite; a program needn't handle non-finite values.
Results may differ from a plain program's by a relative error of at most 0.0049.
Values may be sent and summed in bfloat16 or wider, within the bound.
A program may use at most 64 MiB of HBM per device.

v0:
```python
import functools

import jax
import jax.numpy as jnp
import numpy as np
from jax import lax
from jax.experimental import pallas as pl
from jax.experimental.pallas import tpu as pltpu
from jax.sharding import PartitionSpec as P

LOSS_SCALE = 2048

beta_one = 0.9
beta_two = 0.99
learn_rate = 0.01
adam_eps = 1e-08
step_count = 10.0

f32 = jnp.float32
bf16 = jnp.bfloat16
MESH = pl.DeviceIdType.MESH
LANES = 128
CONV_ROWS = 124
CONV_LANES = 104
WIN = 128


def adam_update(grad, moment, second, master):
    new_moment = beta_one * moment + (1.0 - beta_one) * grad
    new_second = beta_two * second + (1.0 - beta_two) * grad * grad
    update = (
        new_moment
        / (1.0 - beta_one**step_count)
        / (jnp.sqrt(new_second / (1.0 - beta_two**step_count)) + adam_eps)
    )
    return (new_moment, new_second, master - learn_rate * update)


def selection_tables(ch, emb):
    rows = 8 * ch
    repeat_rows = np.zeros((rows, ch), np.float32)
    repeat_rows[np.arange(rows), np.arange(rows) // 8] = 1
    repeat_lanes = np.zeros((ch, 256), np.float32)
    repeat_lanes[np.arange(rows) // 8, np.arange(rows)] = 1
    repeat_emb = np.zeros((emb, 128), np.float32)
    repeat_emb[np.arange(128) // 8, np.arange(128)] = 1
    add_rows = np.zeros((32, rows + 16), np.float32)
    for i in range(ch + 1):
        add_rows[i, 8 * i : 8 * i + 8] = 1
    order = np.zeros((5 * 256, 768), np.float32)
    for a in range(3):
        for c in range(3):
            pair, slot = divmod(a * 3 + c, 2)
            for i in range(ch):
                tile, local = divmod(i, 16)
                for b in range(3):
                    lane = (8 * local + 6 + b + 3 * slot) % 128
                    order[pair * 256 + tile * 128 + lane, i * 27 + a * 9 + b * 3 + c] = 1
    order[2 * 256 + 128 + 8 * 8 + 7, ch * 27] = 1
    emb_order = np.zeros((128, 128), np.float32)
    for e in range(emb):
        emb_order[8 * e + 7, 88 + e] = 1
    place = np.zeros((WIN, 256), np.float32)
    for o in range(ch):
        for k in range(7):
            place[5 * o + k, k * ch + o] = 1
        place[121, 7 * ch + o] = 1
    for i in range(ch + 1):
        place[121 + i // 8, 192 + i] = 1
        place[122 + i // 8, 224 + i] = 1
    tables = (repeat_rows, repeat_lanes, repeat_emb, add_rows, order, emb_order, place)
    return tuple(jnp.asarray(t, bf16) for t in tables)


def dot(lhs, rhs):
    return jnp.dot(lhs, rhs, preferred_element_type=f32)


def dot_nt(lhs, rhs):
    return lax.dot_general(lhs, rhs, (((1,), (1,)), ((), ())), preferred_element_type=f32)


def dot_tn(lhs, rhs):
    return lax.dot_general(lhs, rhs, (((0,), (0,)), ((), ())), preferred_element_type=f32)


def iota(shape, dim):
    return lax.broadcasted_iota(jnp.int32, shape, dim)


def kernel(
    sizes,
    feat_ref, cot_ref, w_ref, bias_ref, headt_ref, rest_ref, master_ref, moment_ref, second_ref,
    rep_rows_ref, rep_lanes_ref, rep_emb_ref, add_ref, order_hbm, emb_order_ref, place_ref,
    igrad_ref, nmom_ref, nsec_ref, nmas_ref, weights_ref,
    rest_v, flat_b, feat_v, cot_v, wband, hband, conv_v, act_v, dpre_v, grad_v, packed_v, stack_v, order_v,
    fh_send, fh_recv, dh_send, dh_recv,
    p1_recv, p1w_send, p1w_recv, sum_v, p2_send, p2_recv, shard_v, p3_send, p3_recv, grad_shard,
    local_sem, fh_ssem, fh_rsem, dh_ssem, dh_rsem,
    p1_ssem, p1_rsem, p1w_ssem, p1w_rsem, p2_ssem, p2_rsem, p3_ssem, p3_rsem,
    b1_ssem, b1_rsem, g_ssem, g_rsem, b2_ssem, b2_rsem, b3_ssem, b3_rsem,
):
    zs, ys, ss, shard_rows, planes, ch, emb = sizes
    rows = 8 * ch
    cells = planes * LANES
    block_rows = ys * shard_rows
    rep = lax.axis_index("rep")
    s = lax.axis_index("slab")
    z = rep // ys
    y = rep % ys

    def at(zz, yy, sl):
        return (zz * ys + yy, sl)

    def remote(src, dst, ssem, rsem, device):
        return pltpu.make_async_remote_copy(
            src_ref=src, dst_ref=dst, send_sem=ssem, recv_sem=rsem, device_id=device, device_id_type=MESH
        )

    rest_copy = pltpu.make_async_copy(rest_ref.at[0], rest_v, local_sem.at[0])
    rest_copy.start()
    order_copy = pltpu.make_async_copy(order_hbm, order_v, local_sem.at[1])
    order_copy.start()

    barrier = pltpu.get_barrier_semaphore()
    for d in range(1, ss):
        pl.semaphore_signal(barrier, inc=1, device_id=at(z, y, (s + d) % ss), device_id_type=MESH)
    for d in range(1, ys):
        pl.semaphore_signal(barrier, inc=1, device_id=at(z, (y + d) % ys, s), device_id_type=MESH)
    for d in range(1, zs):
        pl.semaphore_signal(barrier, inc=1, device_id=at((z + d) % zs, y, s), device_id_type=MESH)

    for p in range(planes):
        plane = feat_ref[:, p].astype(f32).reshape(rows, LANES).astype(bf16)
        feat_v[0:rows, LANES * (p + 1) : LANES * (p + 2)] = plane
        if p == 0:
            fh_send[0] = plane
        if p == planes - 1:
            fh_send[1] = plane
        cot_v[:, LANES * p : LANES * (p + 1)] = cot_ref[:, p].astype(f32).reshape(8 * emb, LANES).astype(bf16)
    feat_v[rows : rows + 16, :] = jnp.ones((16, cells + 2 * LANES), bf16)
    feat_v[rows + 16 : 256, :] = jnp.zeros((256 - rows - 16, cells + 2 * LANES), bf16)

    pl.semaphore_wait(barrier, (ss - 1) + (ys - 1) + (zs - 1))

    def halo(send, recv, ssem, rsem, up):
        source, slot = (1, 0) if up else (0, 1)
        other = (s + 1) % ss if up else (s + ss - 1) % ss
        return remote(send.at[source], recv.at[slot], ssem.at[source], rsem.at[slot], at(z, y, other))

    def start_halo(send, recv, ssem, rsem):
        @pl.when(s < ss - 1)
        def _():
            halo(send, recv, ssem, rsem, True).start()

        @pl.when(s > 0)
        def _():
            halo(send, recv, ssem, rsem, False).start()

        @pl.when(s == 0)
        def _():
            recv[0] = jnp.zeros((rows, LANES), bf16)

        @pl.when(s == ss - 1)
        def _():
            recv[1] = jnp.zeros((rows, LANES), bf16)

    def wait_halo(send, recv, ssem, rsem):
        @pl.when(s < ss - 1)
        def _():
            halo(send, recv, ssem, rsem, True).wait_send()
            halo(send, recv, ssem, rsem, False).wait_recv()

        @pl.when(s > 0)
        def _():
            halo(send, recv, ssem, rsem, False).wait_send()
            halo(send, recv, ssem, rsem, True).wait_recv()

    start_halo(fh_send, fh_recv, fh_ssem, fh_rsem)

    rest_copy.wait()
    first, last = CONV_ROWS // 16, flat_b.shape[0] // 16 - 1
    flat_b[0 : 16 * first, :] = jnp.zeros((16 * first, LANES), bf16)
    lane16 = iota((16, LANES), 1)

    def moved(here, later):
        return pltpu.roll(jnp.where(lane16 >= LANES - CONV_LANES, here, later), CONV_LANES, 1).astype(bf16)

    def rest_rows(at_row, count):
        start = at_row * LANES
        if not isinstance(start, int):
            start = pl.multiple_of(start, LANES)
        return rest_v[0:1, pl.ds(start, count * LANES)].reshape(count, LANES)

    def align(j, carry):
        at_row = j * 16 - CONV_ROWS - 1
        flat_b[pl.ds(pl.multiple_of(j * 16, 16), 16), :] = moved(rest_rows(at_row, 16), rest_rows(at_row + 1, 16))
        return carry

    lead = CONV_ROWS - 16 * first
    start_rows = rest_rows(0, 8)
    flat_b[16 * first : 16 * first + 16, :] = moved(
        jnp.concatenate([jnp.zeros((lead + 1, LANES), f32), start_rows[0 : 15 - lead]], axis=0),
        jnp.concatenate([jnp.zeros((lead, LANES), f32), start_rows[0 : 16 - lead]], axis=0),
    )
    lax.fori_loop(first + 1, last, align, 0)
    end_row = 16 * last - CONV_ROWS - 1
    end = rest_v[0:1, (end_row + 16) * LANES :]
    end = jnp.concatenate([end, jnp.zeros((1, LANES - end.shape[1]), f32)], axis=1)
    end_rows = rest_rows(end_row, 16)
    flat_b[16 * last : 16 * last + 16, :] = moved(end_rows, jnp.concatenate([end_rows[1:16], end], axis=0))

    def p1(d):
        other = (s + d) % ss
        return remote(
            flat_b.at[pl.ds(pl.multiple_of(other * block_rows, 16), block_rows)],
            p1_recv.at[d - 1], p1_ssem.at[d - 1], p1_rsem.at[d - 1], at(z, y, other),
        )

    for d in range(1, ss):
        p1(d).start()

    row = iota((rows, 256), 0)
    lane = iota((rows, 256), 1)
    shift = (lane % 8) - (7 - row % 8)
    spread = dot(w_ref[...].astype(f32).reshape(27 * ch, ch).astype(bf16), rep_lanes_ref[...])
    for a in range(3):
        for c in range(3):
            band = jnp.zeros((rows, 256), f32)
            for b in range(3):
                at_row = (a * 9 + b * 3 + c) * ch
                full = dot(rep_rows_ref[...], spread[at_row : at_row + ch].astype(bf16))
                band = jnp.where(shift == b - 1, full, band)
            wband[a, rows * c : rows * (c + 1), :] = band.astype(bf16)
    head = dot(dot_nt(rep_rows_ref[...], headt_ref[...]).astype(bf16), rep_emb_ref[...])
    hband[...] = jnp.where(shift[:, :LANES] == 0, head, 0.0).astype(bf16)
    bias_row = jnp.concatenate([bias_ref[...], jnp.zeros((1, LANES - ch), f32)], axis=1)
    row_l = iota((rows, LANES), 0)
    lane_l = iota((rows, LANES), 1)
    bias = jnp.sum(jnp.where(lane_l == row_l // 8, jnp.broadcast_to(bias_row, (rows, LANES)), 0.0), axis=1, keepdims=True)

    conv_v[...] = dot(wband[1], feat_v[:, LANES : LANES + cells])
    wait_halo(fh_send, fh_recv, fh_ssem, fh_rsem)
    feat_v[0:rows, 0:LANES] = fh_recv[0]
    feat_v[0:rows, LANES + cells : 2 * LANES + cells] = fh_recv[1]
    conv_v[...] += dot(wband[0], feat_v[:, 0:cells]) + dot(wband[2], feat_v[:, 2 * LANES : 2 * LANES + cells])

    def right(v):
        return jnp.where(lane_l == 0, 0.0, pltpu.roll(v, 1, 1))

    def left(v):
        return jnp.where(lane_l == LANES - 1, 0.0, pltpu.roll(v, LANES - 1, 1))

    def spread_dpre(dpre, p):
        at_lane = slice(LANES * p, LANES * (p + 1))
        dpre_v[0:rows, at_lane] = left(dpre).astype(bf16)
        dpre_v[rows : 2 * rows, at_lane] = dpre.astype(bf16)
        dpre_v[2 * rows : 3 * rows, at_lane] = right(dpre).astype(bf16)

    for p in (0, planes - 1) + tuple(range(1, planes - 1)):
        at_lane = slice(LANES * p, LANES * (p + 1))
        pre = (
            conv_v[rows : 2 * rows, at_lane]
            + right(conv_v[0:rows, at_lane])
            + left(conv_v[2 * rows : 3 * rows, at_lane])
            + bias
        )
        sigma = jax.nn.sigmoid(pre)
        act_v[0:rows, at_lane] = (pre * sigma).astype(bf16)
        dact = dot(hband[...], cot_v[:, at_lane])
        dpre = (dact * sigma * (1.0 + pre * (1.0 - sigma))).astype(bf16)
        if p == 0:
            dh_send[0] = dpre
        if p == planes - 1:
            dh_send[1] = dpre
        spread_dpre(dpre.astype(f32), p + 1)
        if p == planes - 1:
            start_halo(dh_send, dh_recv, dh_ssem, dh_rsem)
    act_v[rows : rows + 16, :] = jnp.ones((16, cells), bf16)

    def p1w(slot):
        return remote(p1w_send, p1w_recv.at[slot], p1w_ssem, p1w_rsem.at[slot], at(z, y, 0))

    def p2(d):
        other = (y + d) % ys
        return remote(
            p2_send.at[pl.ds(pl.multiple_of(other * shard_rows, 16), shard_rows)],
            p2_recv.at[d - 1], p2_ssem.at[d - 1], p2_rsem.at[d - 1], at(z, other, s),
        )

    def p3(slot):
        return remote(p3_send, p3_recv.at[slot], p3_ssem, p3_rsem.at[slot], at(s, y, s))

    def b1(d):
        mine = weights_ref.at[pl.ds(pl.multiple_of(s * block_rows + y * shard_rows, 16), shard_rows)]
        return remote(mine, mine, b1_ssem.at[d - 1], b1_rsem, at((z + d) % zs, y, s))

    def share(d):
        return remote(grad_shard, grad_shard, g_ssem.at[d - 1], g_rsem, at(z, y, (s + d) % ss))

    def b2(d, back):
        owner = (y + ys - d) % ys if back else y
        part = weights_ref.at[pl.ds(pl.multiple_of(s * block_rows + owner * shard_rows, 16), shard_rows)]
        return remote(part, part, b2_ssem.at[d - 1], b2_rsem.at[d - 1], at(z, (y + d) % ys, s))

    def b3(d, back):
        owner = (s + ss - d) % ss if back else s
        part = weights_ref.at[pl.ds(pl.multiple_of(owner * block_rows, 16), block_rows)]
        return remote(part, part, b3_ssem.at[d - 1], b3_rsem.at[d - 1], at(z, y, (s + d) % ss))

    def sum_slabs(with_window):
        for d in range(1, ss):
            p1(d).wait_recv()
        total = flat_b[pl.ds(pl.multiple_of(s * block_rows, 16), block_rows), :].astype(f32)
        for d in range(1, ss):
            total = total + p1_recv[d - 1].astype(f32)
        sum_v[...] = total
        if with_window:
            for d in range(1, ss):
                p1w(d - 1).wait_recv()
            window = p1w_send[...].astype(f32)
            for d in range(1, ss):
                window = window + p1w_recv[d - 1].astype(f32)
            sum_v[0:WIN, :] += window
        p2_send[...] = sum_v[...].astype(bf16)
        for d in range(1, ys):
            p2(d).start()

    def sum_ys():
        for d in range(1, ys):
            p2(d).wait_recv()
        total = sum_v[pl.ds(pl.multiple_of(y * shard_rows, 16), shard_rows), :]
        for d in range(1, ys):
            total = total + p2_recv[d - 1].astype(f32)
        shard_v[...] = total

        @pl.when(z != s)
        def _():
            p3_send[...] = total.astype(bf16)
            p3((s + zs - z - 1) % zs).start()

    def update():
        new_moment, new_second, new_master = adam_update(
            grad_shard[...], moment_ref[...], second_ref[...], master_ref[...]
        )
        nmom_ref[...] = new_moment
        nsec_ref[...] = new_second
        nmas_ref[...] = new_master
        return new_master

    def reduce_shard():
        for d in range(1, zs):
            p3(d - 1).wait_recv()
        total = shard_v[...]
        for d in range(1, zs):
            total = total + p3_recv[d - 1].astype(f32)
        grad_shard[...] = total / LOSS_SCALE
        new_master = update()
        weights_ref[pl.ds(pl.multiple_of(s * block_rows + y * shard_rows, 16), shard_rows), :] = new_master.astype(bf16)
        for d in range(1, zs):
            b1(d).start()
        for d in range(1, ss):
            share(d).start()

    def gather_ys():
        @pl.when(z != s)
        def _():
            b1(1).wait_recv()

        for d in range(1, ys):
            b2(d, False).start()

    def gather_slabs():
        for d in range(1, ys):
            b2(d, True).wait_recv()
        for d in range(1, ss):
            b3(d, False).start()

    early = s != 0
    late = s == 0

    pl.when(early)(lambda: sum_slabs(False))

    mask = ((lane < rows) & (shift >= -1) & (shift <= 1)) | ((lane >= rows) & (lane < rows + 8) & (shift == 0))
    mask = [mask[:, :LANES], mask[:, LANES:]]
    for a in range(3):
        grad_v[a] = dot_nt(dpre_v[:, LANES : LANES + cells], feat_v[:, LANES * a : LANES * a + cells])
    pl.when(early)(sum_ys)
    order_copy.wait()

    def rolled(v, by):
        return jnp.concatenate(
            [pltpu.roll(v[8 * o : 8 * o + 8], by, 1, stride=1, stride_axis=0) for o in range(v.shape[0] // 8)], axis=0
        )

    for pair in range(5):
        for t in range(2):
            total = None
            for slot in range(2):
                if pair * 2 + slot < 9:
                    a, c = divmod(pair * 2 + slot, 3)
                    part = grad_v[a, rows * c : rows * (c + 1), LANES * t : LANES * (t + 1)]
                    part = rolled(jnp.where(mask[t], part, 0.0), 3 * slot)
                    total = part if total is None else total + part
            at_lane = pair * 256 + t * LANES
            packed_v[:, at_lane : at_lane + LANES] = total.astype(bf16)
    sums = dot(add_ref[0:ch, 0:rows], packed_v[...])
    ordered = dot(sums.astype(bf16), order_v[...])
    lane8 = iota((8, LANES), 1)
    row8 = iota((8, LANES), 0)
    zero8 = jnp.zeros((8, LANES), f32)
    for t in range(ch // 8):
        whole, base = divmod(64 * t, LANES)
        by = base + 8 * row8
        tiles = []
        for k in range(6):
            piece = ordered[8 * t : 8 * t + 8, LANES * k : LANES * (k + 1)]
            if k == 5:
                piece = jnp.where(lane8 < 8, piece, 0.0)
            tiles.append(pltpu.roll(piece, base, 1, stride=8, stride_axis=0))
        for m in range(7):
            k = m - whole
            high = tiles[k] if 0 <= k < 6 else zero8
            low = tiles[k - 1] if 0 <= k - 1 < 6 else zero8
            stack_v[m * ch + 8 * t : m * ch + 8 * t + 8, :] = jnp.where(lane8 >= by, high, low)
        bgrad = jnp.broadcast_to(ordered[8 * t : 8 * t + 8, 27 * ch : 27 * ch + 1], (8, LANES))
        stack_v[7 * ch + 8 * t : 7 * ch + 8 * t + 8, :] = jnp.where(lane8 == 64 + 8 * t + row8, bgrad, 0.0)

    hgrad = dot_nt(act_v[...], cot_v[...])
    row_h = iota((rows + 16, LANES), 0)
    lane_h = iota((rows + 16, LANES), 1)
    hgrad = rolled(jnp.where(lane_h % 8 == 7 - row_h % 8, hgrad, 0.0), 0).astype(bf16)
    hgrad = dot(dot(add_ref[...], hgrad).astype(bf16), emb_order_ref[...])
    for t in range(4):
        piece = pltpu.roll(hgrad[8 * t : 8 * t + 8], 0, 1, stride=16, stride_axis=0)
        stack_v[192 + 8 * t : 200 + 8 * t, :] = jnp.where(lane8 >= 88, piece, 0.0)
        stack_v[224 + 8 * t : 232 + 8 * t, :] = jnp.where(lane8 < 88, piece, 0.0)
    p1w_send[...] = dot(place_ref[...], stack_v[...].astype(bf16)).astype(bf16)

    @pl.when(early)
    def _():
        p1w(ss - 1 - s).start()

    reducer = z == s
    pl.when(early & reducer)(reduce_shard)

    wait_halo(dh_send, dh_recv, dh_ssem, dh_rsem)
    spread_dpre(dh_recv[0].astype(f32), 0)
    spread_dpre(dh_recv[1].astype(f32), planes + 1)

    pl.when(late)(lambda: sum_slabs(True))
    pl.when(early)(gather_ys)

    total = None
    for a in range(3):
        part = dot_tn(wband[a, :, 0:rows], dpre_v[:, LANES * (2 - a) : LANES * (2 - a) + cells])
        total = part if total is None else total + part
    for p in range(planes):
        igrad_ref[:, p] = total[:, LANES * p : LANES * (p + 1)].reshape(ch, 8, LANES).astype(bf16)

    pl.when(late)(sum_ys)
    pl.when(early)(gather_slabs)
    pl.when(late & reducer)(reduce_shard)
    pl.when(late)(gather_ys)
    pl.when(late)(gather_slabs)

    @pl.when(jnp.logical_not(reducer))
    def _():
        share(1).wait_recv()
        update()

    for d in range(1, ss):
        b3(d, True).wait_recv()

    for d in range(1, ss):
        p1(d).wait_send()
        b3(d, False).wait_send()
    for d in range(1, ys):
        p2(d).wait_send()
        b2(d, False).wait_send()

    @pl.when(early)
    def _():
        p1w(0).wait_send()

    @pl.when(jnp.logical_not(reducer))
    def _():
        p3(0).wait_send()

    @pl.when(reducer)
    def _():
        for d in range(1, zs):
            b1(d).wait_send()
        for d in range(1, ss):
            share(d).wait_send()


def on_device(
    features, cotangent, conv_weight, conv_bias, head_weight, grad_rest, master, moment, second
):
    ss = lax.axis_size("slab")
    zs = ss
    ys = lax.axis_size("rep") // zs
    ch, planes = features.shape[1], features.shape[2]
    emb = cotangent.shape[1]
    rows = 8 * ch
    cells = planes * LANES
    shard_rows = master.shape[0] // LANES
    block_rows = ys * shard_rows
    all_rows = ss * block_rows
    rest = grad_rest.shape[2]
    sizes = (zs, ys, ss, shard_rows, planes, ch, emb)
    tables = selection_tables(ch, emb)
    vmem = pl.BlockSpec(memory_space=pltpu.VMEM)
    anywhere = pl.BlockSpec(memory_space=pl.ANY)
    dma = pltpu.SemaphoreType.DMA
    shard = jax.ShapeDtypeStruct((shard_rows, LANES), f32)
    outs = pl.pallas_call(
        functools.partial(kernel, sizes),
        out_shape=(
            jax.ShapeDtypeStruct(features.shape[1:], bf16),
            shard,
            shard,
            shard,
            jax.ShapeDtypeStruct((all_rows, LANES), bf16),
        ),
        in_specs=[vmem] * 5 + [anywhere] + [vmem] * 3 + [vmem] * 4 + [anywhere] + [vmem] * 2,
        out_specs=(vmem,) * 5,
        scratch_shapes=[
            pltpu.VMEM((1, rest), f32),
            pltpu.VMEM((all_rows, LANES), bf16),
            pltpu.VMEM((256, cells + 2 * LANES), bf16),
            pltpu.VMEM((8 * emb, cells), bf16),
            pltpu.VMEM((3, 3 * rows, 256), bf16),
            pltpu.VMEM((rows, LANES), bf16),
            pltpu.VMEM((3 * rows, cells), f32),
            pltpu.VMEM((rows + 16, cells), bf16),
            pltpu.VMEM((3 * rows, cells + 2 * LANES), bf16),
            pltpu.VMEM((3, 3 * rows, 256), f32),
            pltpu.VMEM((rows, 5 * 256), bf16),
            pltpu.VMEM((256, LANES), f32),
            pltpu.VMEM((5 * 256, 768), bf16),
            pltpu.VMEM((2, rows, LANES), bf16),
            pltpu.VMEM((2, rows, LANES), bf16),
            pltpu.VMEM((2, rows, LANES), bf16),
            pltpu.VMEM((2, rows, LANES), bf16),
            pltpu.VMEM((ss - 1, block_rows, LANES), bf16),
            pltpu.VMEM((WIN, LANES), bf16),
            pltpu.VMEM((ss - 1, WIN, LANES), bf16),
            pltpu.VMEM((block_rows, LANES), f32),
            pltpu.VMEM((block_rows, LANES), bf16),
            pltpu.VMEM((ys - 1, shard_rows, LANES), bf16),
            pltpu.VMEM((shard_rows, LANES), f32),
            pltpu.VMEM((shard_rows, LANES), bf16),
            pltpu.VMEM((zs - 1, shard_rows, LANES), bf16),
            pltpu.VMEM((shard_rows, LANES), f32),
            dma((2,)),
            dma((2,)), dma((2,)), dma((2,)), dma((2,)),
            dma((ss - 1,)), dma((ss - 1,)),
            dma, dma((ss - 1,)),
            dma((ys - 1,)), dma((ys - 1,)),
            dma, dma((zs - 1,)),
            dma((zs - 1,)), dma,
            dma((ss - 1,)), dma,
            dma((ys - 1,)), dma((ys - 1,)),
            dma((ss - 1,)), dma((ss - 1,)),
        ],
        compiler_params=pltpu.CompilerParams(
            collective_id=0, has_side_effects=True, vmem_limit_bytes=48 << 20
        ),
    )(
        features[0],
        cotangent[0],
        conv_weight.transpose(2, 3, 4, 0, 1).reshape(27, ch, ch),
        conv_bias.reshape(1, ch),
        head_weight.T,
        grad_rest,
        master.reshape(shard_rows, LANES),
        moment.reshape(shard_rows, LANES),
        second.reshape(shard_rows, LANES),
        *tables,
    )
    igrad, new_moment, new_second, new_master, weights = outs
    return (
        igrad[None],
        new_moment.reshape(-1),
        new_second.reshape(-1),
        new_master.reshape(-1),
        weights.reshape(-1),
    )


def solution(mesh):
    return jax.shard_map(
        on_device,
        mesh=mesh,
        in_specs=(
            P("rep", None, "slab", None, None),
            P("rep", None, "slab", None, None),
            P(),
            P(),
            P(),
            P("rep", "slab", None),
            P("rep"),
            P("rep"),
            P("rep"),
        ),
        out_specs=(P("rep", None, "slab", None, None), P("rep"), P("rep"), P("rep"), P()),
        check_vma=False,
    )
```

profile of v0, /device:TPU:69, one launch (start us, length us, event | category | flops | bytes accessed | tf_op | source)
XLA Modules:
  0.0 80.7 jit_solution(11237293735195496654)
XLA Ops:
  0.6 0.0 copy-start
  0.6 1.5 %copy-done = bf16[1280,768]{1,0:T(8,128)(2,1)S(1)} copy-done((bf16[1280,768]{1,0:T(8,128)(2,1)S(1)}, bf16[1280,768]{1,0:T(8,128)(2,1)}, u32[]{:S(2)}) %copy-start) | copy-done | bytes 1966104
  2.2 0.0 copy-start.1
  2.2 1.2 %copy-done.1 = f32[1,1,246168]{2,1,0:T(1,128)S(1)} copy-done((f32[1,1,246168]{2,1,0:T(1,128)S(1)}, f32[1,1,246168]{2,1,0:T(1,128)}, u32[]{:S(2)}) %copy-start.1) | copy-done | bytes 984696
  3.4 0.0 copy-start.2
  3.4 0.9 %copy-done.2 = bf16[1,24,4,8,128]{4,3,2,1,0:T(8,128)(2,1)S(1)} copy-done((bf16[1,24,4,8,128]{4,3,2,1,0:T(8,128)(2,1)S(1)}, bf16[1,24,4,8,128]{4,3,2,1,0:T(8,128)(2,1)}, u32[]{:S(2)}) %copy-start.2) | copy-done | bytes 196632
  4.3 0.0 copy-start.3
  4.3 0.9 %copy-done.3 = bf16[24,24,3,3,3]{1,0,4,3,2:T(8,128)(2,1)S(1)} copy-done((bf16[24,24,3,3,3]{1,0,4,3,2:T(8,128)(2,1)S(1)}, bf16[24,24,3,3,3]{1,0,4,3,2:T(8,128)(2,1)}, u32[]{:S(2)}) %copy-start.3) | copy-done | bytes 31128
  5.2 0.0 copy-start.4
  5.2 0.9 %copy-done.4 = bf16[1,16,4,8,128]{4,3,2,1,0:T(8,128)(2,1)S(1)} copy-done((bf16[1,16,4,8,128]{4,3,2,1,0:T(8,128)(2,1)S(1)}, bf16[1,16,4,8,128]{4,3,2,1,0:T(8,128)(2,1)}, u32[]{:S(2)}) %copy-start.4) | copy-done | bytes 131096
  6.1 0.0 copy-start.5
  6.1 0.8 %copy-done.5 = bf16[128,256]{1,0:T(8,128)(2,1)S(1)} copy-done((bf16[128,256]{1,0:T(8,128)(2,1)S(1)}, bf16[128,256]{1,0:T(8,128)(2,1)}, u32[]{:S(2)}) %copy-start.5) | copy-done | bytes 65560
  7.0 0.0 copy-start.6
  7.0 0.8 copy-done.6
  7.8 0.8 copy-done.7
  8.5 0.0 copy-start.8
  8.5 0.7 copy-done.8
  9.3 0.0 copy-start.9
  9.3 0.7 copy-done.9
  10.0 0.0 copy-start.10
  10.0 0.7 copy-done.10
  10.7 0.7 copy-done.11
  11.4 0.7 copy-done.12
  12.1 0.7 copy-done.13
  12.8 0.7 copy-done.14
  13.5 0.7 copy-done.15
  14.1 63.2 %shard_map.191 = (bf16[24,4,8,128]{3,2,1,0:T(8,128)(2,1)S(1)}, f32[32,128]{1,0:T(8,128)S(1)}, f32[32,128]{1,0:T(8,128)S(1)}, f32[32,128]{1,0:T(8,128)S(1)}, bf16[2048,128]{1,0:T(8,128)(2,1)S(1)}) custom-call(bf16[24,4,8,128]{3,2,1,0:T(8,128)(2,1)S(1)} %bitcast.17, bf16[16,4,8,128]{3,2,1,0:T(8,128)(2,1)S(1)} %bitcast.19, bf16[27,24,24]{2,1,0:T(8,128)(2,1)S(1)} %bitcast.18, ...), custom_call_target="tpu_custom_call" | custom-call | tf_op jit(solution)/shard_map/pallas_call | solution.py:518
  77.3 0.7 copy.26
  78.0 0.6 copy.27
  78.6 0.6 copy.28
  79.2 0.6 copy.29
  79.8 0.8 %copy.30 = bf16[262144]{0:T(1024)(128)(2,1)} copy(bf16[262144]{0:T(1024)(128)(2,1)S(1)} %bitcast.15) | data formatting | bytes 1048576
  (6 shorter events, 0.0 us)
Async XLA Ops:
  0.6 1.5 %copy-start = (bf16[1280,768]{1,0:T(8,128)(2,1)S(1)}, bf16[1280,768]{1,0:T(8,128)(2,1)}, u32[]{:S(2)}) copy-start(bf16[1280,768]{1,0:T(8,128)(2,1)} %constant.18.clone.order_hbm) | copy-start | bytes 5898244
  2.2 1.2 %copy-start.1 = (f32[1,1,246168]{2,1,0:T(1,128)S(1)}, f32[1,1,246168]{2,1,0:T(1,128)}, u32[]{:S(2)}) copy-start(f32[1,1,246168]{2,1,0:T(1,128)} %rest_ref.1) | copy-start | bytes 2954020
  3.4 0.9 %copy-start.2 = (bf16[1,24,4,8,128]{4,3,2,1,0:T(8,128)(2,1)S(1)}, bf16[1,24,4,8,128]{4,3,2,1,0:T(8,128)(2,1)}, u32[]{:S(2)}) copy-start(bf16[1,24,4,8,128]{4,3,2,1,0:T(8,128)(2,1)} %param.16) | copy-start | bytes 589828
  4.3 0.9 %copy-start.3 = (bf16[24,24,3,3,3]{1,0,4,3,2:T(8,128)(2,1)S(1)}, bf16[24,24,3,3,3]{1,0,4,3,2:T(8,128)(2,1)}, u32[]{:S(2)}) copy-start(bf16[24,24,3,3,3]{1,0,4,3,2:T(8,128)(2,1)} %param.18) | copy-start | bytes 93316
  5.2 0.9 %copy-start.4 = (bf16[1,16,4,8,128]{4,3,2,1,0:T(8,128)(2,1)S(1)}, bf16[1,16,4,8,128]{4,3,2,1,0:T(8,128)(2,1)}, u32[]{:S(2)}) copy-start(bf16[1,16,4,8,128]{4,3,2,1,0:T(8,128)(2,1)} %param.17) | copy-start | bytes 393220
  6.1 0.8 %copy-start.5 = (bf16[128,256]{1,0:T(8,128)(2,1)S(1)}, bf16[128,256]{1,0:T(8,128)(2,1)}, u32[]{:S(2)}) copy-start(bf16[128,256]{1,0:T(8,128)(2,1)} %constant.20.clone.place_ref) | copy-start | bytes 196612
  7.0 0.8 copy-start.6
  7.8 0.8 copy-start.7
  8.5 0.7 copy-start.8
  9.3 0.7 copy-start.9
  10.0 0.7 copy-start.10
  10.7 0.7 copy-start.11
  11.4 0.7 copy-start.12
  12.1 0.7 copy-start.13
  12.8 0.7 copy-start.14
  13.5 0.7 copy-start.15
where the time goes:
time: 81.4 us; the launch traced here: 80.7 us
  Pallas kernels  63.2 us (78%)
  local copies, waits for them, and re-layouts  16.8 us (21%)
    pallas_call x1, Pallas kernels, on_device(): pl.pallas_call(functools.partial(kernel, sizes), out_shape=(jax.ShapeDtyp...  63.2 us
    unnamed x37, local copies, waits for them, and re-layouts  16.8 us

commit v1 on v0

--- a/solution.py
+++ b/solution.py
@@ -90,15 +90,21 @@
 
 def kernel(
     sizes,
-    feat_ref, cot_ref, w_ref, bias_ref, headt_ref, rest_ref, master_ref, moment_ref, second_ref,
-    rep_rows_ref, rep_lanes_ref, rep_emb_ref, add_ref, order_hbm, emb_order_ref, place_ref,
-    igrad_ref, nmom_ref, nsec_ref, nmas_ref, weights_ref,
-    rest_v, flat_b, feat_v, cot_v, wband, hband, conv_v, act_v, dpre_v, grad_v, packed_v, stack_v, order_v,
+    feat_in, cot_in, w_in, bias_in, headt_in, rest_in, master_in, moment_in, second_in,
+    rep_rows_in, rep_lanes_in, rep_emb_in, add_in, order_in, emb_order_in, place_in,
+    igrad_out, nmom_out, nsec_out, nmas_out, weights_out,
+    feat_ref, cot_ref, w_ref, bias_ref, headt_ref, rest_v, own_state,
+    rep_rows_ref, rep_lanes_ref, rep_emb_ref, add_ref, order_ref, emb_order_ref, place_ref,
+    igrad_v, shards_v, weights_v,
+    flat_b, feat_v, cot_v, wband, hband, conv_v, act_v, dpre_v, grad_v, packed_v, stack_v,
     fh_send, fh_recv, dh_send, dh_recv,
-    p1_recv, p1w_send, p1w_recv, sum_v, p2_send, p2_recv, shard_v, p3_send, p3_recv, grad_shard,
-    local_sem, fh_ssem, fh_rsem, dh_ssem, dh_rsem,
-    p1_ssem, p1_rsem, p1w_ssem, p1w_rsem, p2_ssem, p2_rsem, p3_ssem, p3_rsem,
-    b1_ssem, b1_rsem, g_ssem, g_rsem, b2_ssem, b2_rsem, b3_ssem, b3_rsem,
+    p1_recv, sum_v, p2_send, p2_recv, p3_all, col_state, grad_shard, own_grad,
+    win_send, win_recv, wy_all, wz_all, win_state, win_grad, win_weights,
+    local_sem, out_sem, fh_ssem, fh_rsem, dh_ssem, dh_rsem,
+    p1_ssem, p1_rsem, p2_ssem, p2_rsem, p3_ssem, p3_rsem,
+    col_ssem, col_rsem, share_ssem, share_rsem, b2_ssem, b2_rsem, b3_ssem, b3_rsem,
+    w1_ssem, w1_rsem, wy_ssem, wy_rsem, wz_ssem, wz_rsem, wb_ssem, wb_rsem,
+    ws_y_ssem, ws_z_ssem, ws_rsem, wshare_ssem, wshare_rsem,
 ):
     zs, ys, ss, shard_rows, planes, ch, emb = sizes
     rows = 8 * ch
@@ -117,10 +123,16 @@
             src_ref=src, dst_ref=dst, send_sem=ssem, recv_sem=rsem, device_id=device, device_id_type=MESH
         )
 
-    rest_copy = pltpu.make_async_copy(rest_ref.at[0], rest_v, local_sem.at[0])
-    rest_copy.start()
-    order_copy = pltpu.make_async_copy(order_hbm, order_v, local_sem.at[1])
-    order_copy.start()
+    ins = (
+        (feat_in, feat_ref), (w_in, w_ref), (rep_lanes_in, rep_lanes_ref), (rep_rows_in, rep_rows_ref),
+        (rest_in.at[0], rest_v), (headt_in, headt_ref), (rep_emb_in, rep_emb_ref), (bias_in, bias_ref),
+        (cot_in, cot_ref), (order_in, order_ref), (add_in, add_ref), (emb_order_in, emb_order_ref),
+        (place_in, place_ref),
+        *[(ref, own_state.at[pl.ds(i * shard_rows, shard_rows)]) for i, ref in enumerate((moment_in, second_in, master_in))],
+    )
+    copies = [pltpu.make_async_copy(src, dst, local_sem.at[i]) for i, (src, dst) in enumerate(ins)]
+    for copy in copies:
+        copy.start()
 
     barrier = pltpu.get_barrier_semaphore()
     for d in range(1, ss):
@@ -130,6 +142,7 @@
     for d in range(1, zs):
         pl.semaphore_signal(barrier, inc=1, device_id=at((z + d) % zs, y, s), device_id_type=MESH)
 
+    copies[0].wait()
     for p in range(planes):
         plane = feat_ref[:, p].astype(f32).reshape(rows, LANES).astype(bf16)
         feat_v[0:rows, LANES * (p + 1) : LANES * (p + 2)] = plane
@@ -137,7 +150,6 @@
             fh_send[0] = plane
         if p == planes - 1:
             fh_send[1] = plane
-        cot_v[:, LANES * p : LANES * (p + 1)] = cot_ref[:, p].astype(f32).reshape(8 * emb, LANES).astype(bf16)
     feat_v[rows : rows + 16, :] = jnp.ones((16, cells + 2 * LANES), bf16)
     feat_v[rows + 16 : 256, :] = jnp.zeros((256 - rows - 16, cells + 2 * LANES), bf16)
 
@@ -178,7 +190,41 @@
 
     start_halo(fh_send, fh_recv, fh_ssem, fh_rsem)
 
-    rest_copy.wait()
+    for i in (13, 14, 15):
+        copies[i].wait()
+    reducer = z == s
+    win_part = WIN // ss
+    win_y = (s * win_part) // shard_rows
+    win_row = (s * win_part) % shard_rows
+    win_source = (z == 0) & (y == win_y)
+
+    def col(d):
+        return remote(own_state, col_state, col_ssem.at[d - 1], col_rsem, at((z + d) % zs, y, s))
+
+    def ws_y(d):
+        return remote(win_state, win_state, ws_y_ssem.at[d - 1], ws_rsem, at(z, (y + d) % ys, s))
+
+    def ws_z(d):
+        return remote(win_state, win_state, ws_z_ssem.at[d - 1], ws_rsem, at((z + d) % zs, y, s))
+
+    @pl.when(reducer)
+    def _():
+        for d in range(1, zs):
+            col(d).start()
+        col_state[...] = own_state[...]
+
+    @pl.when(win_source)
+    def _():
+        for i in range(3):
+            win_state[i * win_part : (i + 1) * win_part, :] = own_state[
+                pl.ds(pl.multiple_of(i * shard_rows + win_row, 16), win_part), :
+            ]
+        for d in range(1, ys):
+            ws_y(d).start()
+        for d in range(1, zs):
+            ws_z(d).start()
+
+    copies[4].wait()
     first, last = CONV_ROWS // 16, flat_b.shape[0] // 16 - 1
     flat_b[0 : 16 * first, :] = jnp.zeros((16 * first, LANES), bf16)
     lane16 = iota((16, LANES), 1)
@@ -223,6 +269,10 @@
     row = iota((rows, 256), 0)
     lane = iota((rows, 256), 1)
     shift = (lane % 8) - (7 - row % 8)
+    for i in (1, 2, 3, 5, 6, 7, 8):
+        copies[i].wait()
+    for p in range(planes):
+        cot_v[:, LANES * p : LANES * (p + 1)] = cot_ref[:, p].astype(f32).reshape(8 * emb, LANES).astype(bf16)
     spread = dot(w_ref[...].astype(f32).reshape(27 * ch, ch).astype(bf16), rep_lanes_ref[...])
     for a in range(3):
         for c in range(3):
@@ -278,9 +328,6 @@
             start_halo(dh_send, dh_recv, dh_ssem, dh_rsem)
     act_v[rows : rows + 16, :] = jnp.ones((16, cells), bf16)
 
-    def p1w(slot):
-        return remote(p1w_send, p1w_recv.at[slot], p1w_ssem, p1w_rsem.at[slot], at(z, y, 0))
-
     def p2(d):
         other = (y + d) % ys
         return remote(
@@ -288,105 +335,177 @@
             p2_recv.at[d - 1], p2_ssem.at[d - 1], p2_rsem.at[d - 1], at(z, other, s),
         )
 
-    def p3(slot):
-        return remote(p3_send, p3_recv.at[slot], p3_ssem, p3_rsem.at[slot], at(s, y, s))
-
-    def b1(d):
-        mine = weights_ref.at[pl.ds(pl.multiple_of(s * block_rows + y * shard_rows, 16), shard_rows)]
-        return remote(mine, mine, b1_ssem.at[d - 1], b1_rsem, at((z + d) % zs, y, s))
+    def p3(d, back):
+        part = p3_all.at[(z + zs - d) % zs if back else z]
+        return remote(part, part, p3_ssem.at[d - 1], p3_rsem.at[d - 1], at((z + d) % zs, y, s))
 
     def share(d):
-        return remote(grad_shard, grad_shard, g_ssem.at[d - 1], g_rsem, at(z, y, (s + d) % ss))
+        return remote(grad_shard, grad_shard, share_ssem.at[d - 1], share_rsem, at(z, y, (s + d) % ss))
 
     def b2(d, back):
         owner = (y + ys - d) % ys if back else y
-        part = weights_ref.at[pl.ds(pl.multiple_of(s * block_rows + owner * shard_rows, 16), shard_rows)]
+        part = weights_v.at[pl.ds(pl.multiple_of(s * block_rows + owner * shard_rows, 16), shard_rows)]
         return remote(part, part, b2_ssem.at[d - 1], b2_rsem.at[d - 1], at(z, (y + d) % ys, s))
 
     def b3(d, back):
         owner = (s + ss - d) % ss if back else s
-        part = weights_ref.at[pl.ds(pl.multiple_of(owner * block_rows, 16), block_rows)]
+        part = weights_v.at[pl.ds(pl.multiple_of(owner * block_rows, 16), block_rows)]
         return remote(part, part, b3_ssem.at[d - 1], b3_rsem.at[d - 1], at(z, y, (s + d) % ss))
 
-    def sum_slabs(with_window):
+    def w1(d):
+        part = win_send.at[pl.ds(pl.multiple_of((s + d) % ss * win_part, 16), win_part)]
+        return remote(part, win_recv.at[d - 1], w1_ssem.at[d - 1], w1_rsem.at[d - 1], at(z, y, (s + d) % ss))
+
+    def wy(d, back):
+        part = wy_all.at[(y + ys - d) % ys if back else y]
+        return remote(part, part, wy_ssem.at[d - 1], wy_rsem.at[d - 1], at(z, (y + d) % ys, s))
+
+    def wz(d, back):
+        part = wz_all.at[(z + zs - d) % zs if back else z]
+        return remote(part, part, wz_ssem.at[d - 1], wz_rsem.at[d - 1], at((z + d) % zs, y, s))
+
+    def wb(d, back):
+        owner = (s + ss - d) % ss if back else s
+        part = win_weights.at[pl.ds(pl.multiple_of(owner * win_part, 16), win_part)]
+        return remote(part, part, wb_ssem.at[d - 1], wb_rsem.at[d - 1], at(z, y, (s + d) % ss))
+
+    per_shard = shard_rows // win_part
+
+    def wshare(d):
+        part = win_grad.at[s % per_shard]
+        return remote(part, part, wshare_ssem.at[d - 1], wshare_rsem.at[s % per_shard], at(z, y, (s + d) % ss))
+
+    def updated(grad, state):
+        count = grad.shape[0]
+        return adam_update(grad, state[0:count, :], state[count : 2 * count, :], state[2 * count : 3 * count, :])
+
+    def start_ys():
         for d in range(1, ss):
             p1(d).wait_recv()
         total = flat_b[pl.ds(pl.multiple_of(s * block_rows, 16), block_rows), :].astype(f32)
         for d in range(1, ss):
             total = total + p1_recv[d - 1].astype(f32)
         sum_v[...] = total
-        if with_window:
-            for d in range(1, ss):
-                p1w(d - 1).wait_recv()
-            window = p1w_send[...].astype(f32)
-            for d in range(1, ss):
-                window = window + p1w_recv[d - 1].astype(f32)
-            sum_v[0:WIN, :] += window
-        p2_send[...] = sum_v[...].astype(bf16)
+        p2_send[...] = total.astype(bf16)
         for d in range(1, ys):
             p2(d).start()
 
-    def sum_ys():
+    def start_zs():
         for d in range(1, ys):
             p2(d).wait_recv()
         total = sum_v[pl.ds(pl.multiple_of(y * shard_rows, 16), shard_rows), :]
         for d in range(1, ys):
             total = total + p2_recv[d - 1].astype(f32)
-        shard_v[...] = total
-
-        @pl.when(z != s)
-        def _():
-            p3_send[...] = total.astype(bf16)
-            p3((s + zs - z - 1) % zs).start()
-
-    def update():
-        new_moment, new_second, new_master = adam_update(
-            grad_shard[...], moment_ref[...], second_ref[...], master_ref[...]
-        )
-        nmom_ref[...] = new_moment
-        nsec_ref[...] = new_second
-        nmas_ref[...] = new_master
-        return new_master
-
-    def reduce_shard():
-        for d in range(1, zs):
-            p3(d - 1).wait_recv()
-        total = shard_v[...]
-        for d in range(1, zs):
-            total = total + p3_recv[d - 1].astype(f32)
-        grad_shard[...] = total / LOSS_SCALE
-        new_master = update()
-        weights_ref[pl.ds(pl.multiple_of(s * block_rows + y * shard_rows, 16), shard_rows), :] = new_master.astype(bf16)
-        for d in range(1, zs):
-            b1(d).start()
-        for d in range(1, ss):
-            share(d).start()
-
-    def gather_ys():
-        @pl.when(z != s)
-        def _():
-            b1(1).wait_recv()
-
+        p3_all[z] = total.astype(bf16)
+        for d in range(1, zs):
+            p3(d, False).start()
+
+    def start_gather_ys():
+        @pl.when(jnp.logical_not(reducer))
+        def _():
+            col(1).wait_recv()
+
+        for d in range(1, zs):
+            p3(d, True).wait_recv()
+        grad = p3_all[0].astype(f32)
+        for i in range(1, zs):
+            grad = grad + p3_all[i].astype(f32)
+        grad = grad / LOSS_SCALE
+        weights = updated(grad, col_state)[2].astype(bf16)
+        weights_v[pl.ds(pl.multiple_of(s * block_rows + y * shard_rows, 16), shard_rows), :] = weights
         for d in range(1, ys):
             b2(d, False).start()
 
-    def gather_slabs():
+        @pl.when(reducer)
+        def _():
+            grad_shard[...] = grad
+            for d in range(1, ss):
+                share(d).start()
+
+    def start_gather_slabs():
         for d in range(1, ys):
             b2(d, True).wait_recv()
         for d in range(1, ss):
             b3(d, False).start()
 
-    early = s != 0
-    late = s == 0
-
-    pl.when(early)(lambda: sum_slabs(False))
+    def start_window_ys():
+        for d in range(1, ss):
+            w1(d).wait_recv()
+        total = win_send[pl.ds(pl.multiple_of(s * win_part, 16), win_part), :].astype(f32)
+        for d in range(1, ss):
+            total = total + win_recv[d - 1].astype(f32)
+        wy_all[y] = total.astype(bf16)
+        for d in range(1, ys):
+            wy(d, False).start()
+
+    def start_window_zs():
+        for d in range(1, ys):
+            wy(d, True).wait_recv()
+        total = wy_all[0].astype(f32)
+        for i in range(1, ys):
+            total = total + wy_all[i].astype(f32)
+        wz_all[z] = total.astype(bf16)
+        for d in range(1, zs):
+            wz(d, False).start()
+
+    in_window = (z == 0) & (y < WIN // shard_rows)
+    win_owner = (z == 0) & (y == win_y)
+
+    def start_window_gather():
+        for d in range(1, zs):
+            wz(d, True).wait_recv()
+        grad = wz_all[0].astype(f32)
+        for i in range(1, zs):
+            grad = grad + wz_all[i].astype(f32)
+        grad = grad / LOSS_SCALE
+        weights = updated(grad, win_state)[2].astype(bf16)
+        win_weights[pl.ds(pl.multiple_of(s * win_part, 16), win_part), :] = weights
+        for d in range(1, ss):
+            wb(d, False).start()
+
+        @pl.when(win_owner)
+        def _():
+            win_grad[s % per_shard] = grad
+            for d in range(1, ss):
+                wshare(d).start()
+
+    def finish_window():
+        for d in range(1, ss):
+            wb(d, True).wait_recv()
+
+    def own_update():
+        @pl.when(jnp.logical_not(reducer))
+        def _():
+            share(1).wait_recv()
+
+        own_grad[...] = grad_shard[...]
+
+        @pl.when(in_window)
+        def _():
+            for i in range(per_shard):
+                @pl.when(s != y * per_shard + i)
+                def _():
+                    part = win_grad.at[i]
+                    remote(part, part, wshare_ssem.at[0], wshare_rsem.at[i], at(z, y, (s + 1) % ss)).wait_recv()
+
+                own_grad[i * win_part : (i + 1) * win_part, :] = win_grad[i]
+
+        for i, value in enumerate(updated(own_grad[...], own_state)):
+            shards_v[i] = value
+
+    outs = [pltpu.make_async_copy(igrad_v, igrad_out, out_sem.at[0])]
+    outs += [
+        pltpu.make_async_copy(shards_v.at[i], ref, out_sem.at[1 + i]) for i, ref in enumerate((nmom_out, nsec_out, nmas_out))
+    ]
+    outs += [pltpu.make_async_copy(weights_v, weights_out, out_sem.at[4])]
 
     mask = ((lane < rows) & (shift >= -1) & (shift <= 1)) | ((lane >= rows) & (lane < rows + 8) & (shift == 0))
     mask = [mask[:, :LANES], mask[:, LANES:]]
     for a in range(3):
         grad_v[a] = dot_nt(dpre_v[:, LANES : LANES + cells], feat_v[:, LANES * a : LANES * a + cells])
-    pl.when(early)(sum_ys)
-    order_copy.wait()
+    start_ys()
+    for i in range(9, 13):
+        copies[i].wait()
 
     def rolled(v, by):
         return jnp.concatenate(
@@ -405,7 +524,7 @@
             at_lane = pair * 256 + t * LANES
             packed_v[:, at_lane : at_lane + LANES] = total.astype(bf16)
     sums = dot(add_ref[0:ch, 0:rows], packed_v[...])
-    ordered = dot(sums.astype(bf16), order_v[...])
+    ordered = dot(sums.astype(bf16), order_ref[...])
     lane8 = iota((8, LANES), 1)
     row8 = iota((8, LANES), 0)
     zero8 = jnp.zeros((8, LANES), f32)
@@ -435,64 +554,102 @@
         piece = pltpu.roll(hgrad[8 * t : 8 * t + 8], 0, 1, stride=16, stride_axis=0)
         stack_v[192 + 8 * t : 200 + 8 * t, :] = jnp.where(lane8 >= 88, piece, 0.0)
         stack_v[224 + 8 * t : 232 + 8 * t, :] = jnp.where(lane8 < 88, piece, 0.0)
-    p1w_send[...] = dot(place_ref[...], stack_v[...].astype(bf16)).astype(bf16)
-
-    @pl.when(early)
+    window = dot(place_ref[...], stack_v[...].astype(bf16)) + flat_b[0:WIN, :].astype(f32)
+    win_send[...] = window.astype(bf16)
+    for d in range(1, ss):
+        w1(d).start()
+
+    @pl.when((z == 0) & (y != win_y))
     def _():
-        p1w(ss - 1 - s).start()
-
-    reducer = z == s
-    pl.when(early & reducer)(reduce_shard)
+        ws_y(1).wait_recv()
+        for d in range(1, zs):
+            ws_z(d).start()
+
+    start_zs()
 
     wait_halo(dh_send, dh_recv, dh_ssem, dh_rsem)
     spread_dpre(dh_recv[0].astype(f32), 0)
     spread_dpre(dh_recv[1].astype(f32), planes + 1)
-
-    pl.when(late)(lambda: sum_slabs(True))
-    pl.when(early)(gather_ys)
 
     total = None
     for a in range(3):
         part = dot_tn(wband[a, :, 0:rows], dpre_v[:, LANES * (2 - a) : LANES * (2 - a) + cells])
         total = part if total is None else total + part
     for p in range(planes):
-        igrad_ref[:, p] = total[:, LANES * p : LANES * (p + 1)].reshape(ch, 8, LANES).astype(bf16)
-
-    pl.when(late)(sum_ys)
-    pl.when(early)(gather_slabs)
-    pl.when(late & reducer)(reduce_shard)
-    pl.when(late)(gather_ys)
-    pl.when(late)(gather_slabs)
-
-    @pl.when(jnp.logical_not(reducer))
+        igrad_v[:, p] = total[:, LANES * p : LANES * (p + 1)].reshape(ch, 8, LANES).astype(bf16)
+    outs[0].start()
+
+    start_window_ys()
+    start_gather_ys()
+    start_window_zs()
+    start_gather_slabs()
+    @pl.when(z != 0)
     def _():
-        share(1).wait_recv()
-        update()
-
+        ws_z(1).wait_recv()
+
+    start_window_gather()
+    own_update()
+    for out in outs[1:4]:
+        out.start()
+    finish_window()
     for d in range(1, ss):
         b3(d, True).wait_recv()
+    for d in range(1, ss):
+        b3(d, False).wait_send()
+    for d in range(1, ys):
+        b2(d, False).wait_send()
+    weights_v[0:WIN, :] = win_weights[...]
+    outs[4].start()
 
     for d in range(1, ss):
         p1(d).wait_send()
-        b3(d, False).wait_send()
+        w1(d).wait_send()
+        wb(d, False).wait_send()
     for d in range(1, ys):
         p2(d).wait_send()
-        b2(d, False).wait_send()
-
-    @pl.when(early)
-    def _():
-        p1w(0).wait_send()
-
-    @pl.when(jnp.logical_not(reducer))
-    def _():
-        p3(0).wait_send()
+        wy(d, False).wait_send()
+    for d in range(1, zs):
+        p3(d, False).wait_send()
+        wz(d, False).wait_send()
 
     @pl.when(reducer)
     def _():
         for d in range(1, zs):
-            b1(d).wait_send()
+            col(d).wait_send()
         for d in range(1, ss):
             share(d).wait_send()
+
+    @pl.when(win_source)
+    def _():
+        for d in range(1, ys):
+            ws_y(d).wait_send()
+
+    @pl.when(z == 0)
+    def _():
+        for d in range(1, zs):
+            ws_z(d).wait_send()
+
+    @pl.when(win_owner)
+    def _():
+        for d in range(1, ss):
+            wshare(d).wait_send()
+
+    for out in outs:
+        out.wait()
+
+
+def copy_kernel(*refs):
+    count = (len(refs) - 2) // 3
+    in_sem, out_sem = refs[3 * count :]
+    loads = [pltpu.make_async_copy(refs[i], refs[2 * count + i], in_sem.at[i]) for i in range(count)]
+    stores = [pltpu.make_async_copy(refs[2 * count + i], refs[count + i], out_sem.at[i]) for i in range(count)]
+    for load in loads:
+        load.start()
+    for load, store in zip(loads, stores):
+        load.wait()
+        store.start()
+    for store in stores:
+        store.wait()
 
 
 def on_device(
@@ -508,11 +665,11 @@
     shard_rows = master.shape[0] // LANES
     block_rows = ys * shard_rows
     all_rows = ss * block_rows
+    win_part = WIN // ss
     rest = grad_rest.shape[2]
     sizes = (zs, ys, ss, shard_rows, planes, ch, emb)
     tables = selection_tables(ch, emb)
-    vmem = pl.BlockSpec(memory_space=pltpu.VMEM)
-    anywhere = pl.BlockSpec(memory_space=pl.ANY)
+    hbm = pl.BlockSpec(memory_space=pltpu.HBM)
     dma = pltpu.SemaphoreType.DMA
     shard = jax.ShapeDtypeStruct((shard_rows, LANES), f32)
     outs = pl.pallas_call(
@@ -524,10 +681,20 @@
             shard,
             jax.ShapeDtypeStruct((all_rows, LANES), bf16),
         ),
-        in_specs=[vmem] * 5 + [anywhere] + [vmem] * 3 + [vmem] * 4 + [anywhere] + [vmem] * 2,
-        out_specs=(vmem,) * 5,
+        in_specs=[hbm] * 16,
+        out_specs=(hbm,) * 5,
         scratch_shapes=[
+            pltpu.VMEM(features.shape[1:], bf16),
+            pltpu.VMEM(cotangent.shape[1:], bf16),
+            pltpu.VMEM((27, ch, ch), bf16),
+            pltpu.VMEM((1, ch), f32),
+            pltpu.VMEM((emb, ch), bf16),
             pltpu.VMEM((1, rest), f32),
+            pltpu.VMEM((3 * shard_rows, LANES), f32),
+            *[pltpu.VMEM(t.shape, bf16) for t in tables],
+            pltpu.VMEM(features.shape[1:], bf16),
+            pltpu.VMEM((3, shard_rows, LANES), f32),
+            pltpu.VMEM((all_rows, LANES), bf16),
             pltpu.VMEM((all_rows, LANES), bf16),
             pltpu.VMEM((256, cells + 2 * LANES), bf16),
             pltpu.VMEM((8 * emb, cells), bf16),
@@ -539,34 +706,43 @@
             pltpu.VMEM((3, 3 * rows, 256), f32),
             pltpu.VMEM((rows, 5 * 256), bf16),
             pltpu.VMEM((256, LANES), f32),
-            pltpu.VMEM((5 * 256, 768), bf16),
             pltpu.VMEM((2, rows, LANES), bf16),
             pltpu.VMEM((2, rows, LANES), bf16),
             pltpu.VMEM((2, rows, LANES), bf16),
             pltpu.VMEM((2, rows, LANES), bf16),
             pltpu.VMEM((ss - 1, block_rows, LANES), bf16),
-            pltpu.VMEM((WIN, LANES), bf16),
-            pltpu.VMEM((ss - 1, WIN, LANES), bf16),
             pltpu.VMEM((block_rows, LANES), f32),
             pltpu.VMEM((block_rows, LANES), bf16),
             pltpu.VMEM((ys - 1, shard_rows, LANES), bf16),
+            pltpu.VMEM((zs, shard_rows, LANES), bf16),
+            pltpu.VMEM((3 * shard_rows, LANES), f32),
             pltpu.VMEM((shard_rows, LANES), f32),
-            pltpu.VMEM((shard_rows, LANES), bf16),
-            pltpu.VMEM((zs - 1, shard_rows, LANES), bf16),
             pltpu.VMEM((shard_rows, LANES), f32),
-            dma((2,)),
+            pltpu.VMEM((WIN, LANES), bf16),
+            pltpu.VMEM((ss - 1, win_part, LANES), bf16),
+            pltpu.VMEM((ys, win_part, LANES), bf16),
+            pltpu.VMEM((zs, win_part, LANES), bf16),
+            pltpu.VMEM((3 * win_part, LANES), f32),
+            pltpu.VMEM((shard_rows // win_part, win_part, LANES), f32),
+            pltpu.VMEM((WIN, LANES), bf16),
+            dma((16,)), dma((5,)),
             dma((2,)), dma((2,)), dma((2,)), dma((2,)),
             dma((ss - 1,)), dma((ss - 1,)),
-            dma, dma((ss - 1,)),
             dma((ys - 1,)), dma((ys - 1,)),
-            dma, dma((zs - 1,)),
+            dma((zs - 1,)), dma((zs - 1,)),
             dma((zs - 1,)), dma,
             dma((ss - 1,)), dma,
             dma((ys - 1,)), dma((ys - 1,)),
             dma((ss - 1,)), dma((ss - 1,)),
+            dma((ss - 1,)), dma((ss - 1,)),
+            dma((ys - 1,)), dma((ys - 1,)),
+            dma((zs - 1,)), dma((zs - 1,)),
+            dma((ss - 1,)), dma((ss - 1,)),
+            dma((ys - 1,)), dma((zs - 1,)), dma,
+            dma((ss - 1,)), dma((shard_rows // win_part,)),
         ],
         compiler_params=pltpu.CompilerParams(
-            collective_id=0, has_side_effects=True, vmem_limit_bytes=48 << 20
+            collective_id=0, has_side_effects=True, vmem_limit_bytes=60 << 20
         ),
     )(
         features[0],
@@ -580,7 +756,14 @@
         second.reshape(shard_rows, LANES),
         *tables,
     )
-    igrad, new_moment, new_second, new_master, weights = outs
+    igrad, new_moment, new_second, new_master, weights = pl.pallas_call(
+        copy_kernel,
+        out_shape=tuple(jax.ShapeDtypeStruct(out.shape, out.dtype) for out in outs),
+        in_specs=[pl.BlockSpec(memory_space=pl.ANY)] * 5,
+        out_specs=(pl.BlockSpec(memory_space=pl.ANY),) * 5,
+        scratch_shapes=[pltpu.VMEM(out.shape, out.dtype) for out in outs] + [dma((5,)), dma((5,))],
+        compiler_params=pltpu.CompilerParams(vmem_limit_bytes=60 << 20),
+    )(*outs)
     return (
         igrad[None],
         new_moment.reshape(-1),

time: 81.4 us -> 58.3 us (0.72)
  the two profiles are of different devices: /device:TPU:69 before, /device:TPU:1 now
where the time goes in v1:
time: 58.3 us; the launch traced here: 57.7 us
  Pallas kernels  57 us (98%)
  between operations  0.64 us (1%)
    pallas_call x1, Pallas kernels, on_device(): pl.pallas_call(functools.partial(kernel, sizes), out_shape=(jax.ShapeDtyp...  54.9 us
    pallas_call x1, Pallas kernels, on_device(): pl.pallas_call(copy_kernel, out_shape=tuple((jax.ShapeDtypeStruct(out.sha...  2.08 us

profile of v1, /device:TPU:1, one launch (start us, length us, event | category | flops | bytes accessed | tf_op | source)
XLA Modules:
  0.0 57.7 jit_solution(18428696180804427484)
XLA Ops:
  0.6 54.9 %shard_map.191 = (bf16[24,4,8,128]{3,2,1,0:T(8,128)(2,1)}, f32[32,128]{1,0:T(8,128)}, f32[32,128]{1,0:T(8,128)}, f32[32,128]{1,0:T(8,128)}, bf16[2048,128]{1,0:T(8,128)(2,1)}) custom-call(bf16[24,4,8,128]{3,2,1,0:T(8,128)(2,1)} %bitcast.15, bf16[16,4,8,128]{3,2,1,0:T(8,128)(2,1)} %bitcast.17, bf16[27,24,24]{2,1,0:T(8,128)(2,1)} %bitcast.16, ...), custom_call_target="tpu_custom_call" | custom-call | tf_op jit(solution)/shard_map/pallas_call | solution.py:675
  55.6 2.1 %shard_map.192 = (bf16[24,4,8,128]{3,2,1,0:T(8,128)(2,1)}, f32[32,128]{1,0:T(8,128)}, f32[32,128]{1,0:T(8,128)}, f32[32,128]{1,0:T(8,128)}, bf16[2048,128]{1,0:T(8,128)(2,1)}) custom-call(bf16[24,4,8,128]{3,2,1,0:T(8,128)(2,1)} %get-tuple-element.15.refs_0_, f32[32,128]{1,0:T(8,128)} %get-tuple-element.16.refs_1_, f32[32,128]{1,0:T(8,128)} %get-tuple-element.17.refs_2_, ...), custom_call_target="tpu_custom_call" | custom-call | tf_op jit(solution)/shard_map/pallas_call | solution.py:759

commit v2 on v1

--- a/solution.py
+++ b/solution.py
@@ -93,16 +93,16 @@
     feat_in, cot_in, w_in, bias_in, headt_in, rest_in, master_in, moment_in, second_in,
     rep_rows_in, rep_lanes_in, rep_emb_in, add_in, order_in, emb_order_in, place_in,
     igrad_out, nmom_out, nsec_out, nmas_out, weights_out,
-    feat_ref, cot_ref, w_ref, bias_ref, headt_ref, rest_v, own_state,
+    feat_ref, cot_ref, w_ref, bias_ref, headt_ref, rest_1d, own_state,
     rep_rows_ref, rep_lanes_ref, rep_emb_ref, add_ref, order_ref, emb_order_ref, place_ref,
     igrad_v, shards_v, weights_v,
     flat_b, feat_v, cot_v, wband, hband, conv_v, act_v, dpre_v, grad_v, packed_v, stack_v,
     fh_send, fh_recv, dh_send, dh_recv,
-    p1_recv, sum_v, p2_send, p2_recv, p3_all, col_state, grad_shard, own_grad,
+    p1a_recv, pair_sum, p1b_recv, sum_v, p2_send, p2_recv, p3_all, col_state, grad_shard, own_grad,
     win_send, win_recv, wy_all, wz_all, win_state, win_grad, win_weights,
     local_sem, out_sem, fh_ssem, fh_rsem, dh_ssem, dh_rsem,
-    p1_ssem, p1_rsem, p2_ssem, p2_rsem, p3_ssem, p3_rsem,
-    col_ssem, col_rsem, share_ssem, share_rsem, b2_ssem, b2_rsem, b3_ssem, b3_rsem,
+    p1a_ssem, p1a_rsem, p1b_ssem, p1b_rsem, p2_ssem, p2_rsem, p3_ssem, p3_rsem,
+    col_ssem, col_rsem, share_ssem, share_rsem, b2_ssem, b2_rsem, b3x_ssem, b3x_rsem, b3c_ssem, b3c_rsem,
     w1_ssem, w1_rsem, wy_ssem, wy_rsem, wz_ssem, wz_rsem, wb_ssem, wb_rsem,
     ws_y_ssem, ws_z_ssem, ws_rsem, wshare_ssem, wshare_rsem,
 ):
@@ -123,9 +123,17 @@
             src_ref=src, dst_ref=dst, send_sem=ssem, recv_sem=rsem, device_id=device, device_id_type=MESH
         )
 
+    barrier = pltpu.get_barrier_semaphore()
+    for d in range(1, ss):
+        pl.semaphore_signal(barrier, inc=1, device_id=at(z, y, (s + d) % ss), device_id_type=MESH)
+    for d in range(1, ys):
+        pl.semaphore_signal(barrier, inc=1, device_id=at(z, (y + d) % ys, s), device_id_type=MESH)
+    for d in range(1, zs):
+        pl.semaphore_signal(barrier, inc=1, device_id=at((z + d) % zs, y, s), device_id_type=MESH)
+
     ins = (
         (feat_in, feat_ref), (w_in, w_ref), (rep_lanes_in, rep_lanes_ref), (rep_rows_in, rep_rows_ref),
-        (rest_in.at[0], rest_v), (headt_in, headt_ref), (rep_emb_in, rep_emb_ref), (bias_in, bias_ref),
+        (rest_in.at[0], rest_1d), (headt_in, headt_ref), (rep_emb_in, rep_emb_ref), (bias_in, bias_ref),
         (cot_in, cot_ref), (order_in, order_ref), (add_in, add_ref), (emb_order_in, emb_order_ref),
         (place_in, place_ref),
         *[(ref, own_state.at[pl.ds(i * shard_rows, shard_rows)]) for i, ref in enumerate((moment_in, second_in, master_in))],
@@ -134,13 +142,53 @@
     for copy in copies:
         copy.start()
 
-    barrier = pltpu.get_barrier_semaphore()
-    for d in range(1, ss):
-        pl.semaphore_signal(barrier, inc=1, device_id=at(z, y, (s + d) % ss), device_id_type=MESH)
-    for d in range(1, ys):
-        pl.semaphore_signal(barrier, inc=1, device_id=at(z, (y + d) % ys, s), device_id_type=MESH)
-    for d in range(1, zs):
-        pl.semaphore_signal(barrier, inc=1, device_id=at((z + d) % zs, y, s), device_id_type=MESH)
+    copies[4].wait()
+    first, last = CONV_ROWS // 16, flat_b.shape[0] // 16 - 1
+    flat_b[0 : 16 * first, :] = jnp.zeros((16 * first, LANES), bf16)
+    lane16 = iota((16, LANES), 1)
+
+    def moved(here, later):
+        return pltpu.roll(jnp.where(lane16 >= LANES - CONV_LANES, here, later), CONV_LANES, 1).astype(bf16)
+
+    def rest_rows(start, count):
+        return rest_1d[0:1, pl.ds(start, count * LANES)].reshape(count, LANES)
+
+    lane8 = iota((8, LANES), 1)
+
+    def moved8(here, later):
+        return pltpu.roll(jnp.where(lane8 >= LANES - CONV_LANES, here, later), CONV_LANES, 1)
+
+    per_step = 8
+    skipped = (16 * (first + 1) - CONV_ROWS - 1) * LANES
+
+    def align_at(at_row):
+        halves = []
+        for h in range(2):
+            start = (at_row + 8 * h) * LANES + skipped
+            halves.append(moved8(rest_rows(start, 8), rest_rows(start + LANES, 8)))
+        part = jnp.concatenate(halves, axis=0).astype(bf16)
+        flat_b[pl.ds(at_row + 16 * (first + 1), 16), :] = part
+
+    def align(j, carry):
+        for i in range(per_step):
+            align_at(pl.multiple_of(j * (16 * per_step), 16 * per_step) + 16 * i)
+        return carry
+
+    steps = (last - first - 1) // per_step
+    lax.fori_loop(0, steps, align, 0)
+    for j in range(steps * per_step, last - first - 1):
+        align_at(16 * j)
+    lead = CONV_ROWS - 16 * first
+    start_rows = rest_rows(0, 8)
+    flat_b[16 * first : 16 * first + 16, :] = moved(
+        jnp.concatenate([jnp.zeros((lead + 1, LANES), f32), start_rows[0 : 15 - lead]], axis=0),
+        jnp.concatenate([jnp.zeros((lead, LANES), f32), start_rows[0 : 16 - lead]], axis=0),
+    )
+    end_row = 16 * last - CONV_ROWS - 1
+    end = rest_1d[0:1, (end_row + 16) * LANES :]
+    end = jnp.concatenate([end, jnp.zeros((1, LANES - end.shape[1]), f32)], axis=1)
+    end_rows = rest_rows(end_row * LANES, 16)
+    flat_b[16 * last : 16 * last + 16, :] = moved(end_rows, jnp.concatenate([end_rows[1:16], end], axis=0))
 
     copies[0].wait()
     for p in range(planes):
@@ -155,6 +203,27 @@
 
     pl.semaphore_wait(barrier, (ss - 1) + (ys - 1) + (zs - 1))
 
+    xs = ss // 2
+    x = s // 2
+    core = s % 2
+
+    def block(ref, xx, cc):
+        return ref.at[pl.ds(pl.multiple_of((xx * 2 + cc) * block_rows, 16), block_rows)]
+
+    def p1a(i):
+        return remote(
+            block(flat_b, i, 1 - core), p1a_recv.at[i], p1a_ssem.at[i], p1a_rsem.at[i], at(z, y, x * 2 + 1 - core)
+        )
+
+    def p1b(d):
+        to = (x + d) % xs
+        return remote(
+            pair_sum.at[to], p1b_recv.at[d - 1], p1b_ssem.at[d - 1], p1b_rsem.at[d - 1], at(z, y, to * 2 + core)
+        )
+
+    for i in range(xs):
+        p1a(i).start()
+
     def halo(send, recv, ssem, rsem, up):
         source, slot = (1, 0) if up else (0, 1)
         other = (s + 1) % ss if up else (s + ss - 1) % ss
@@ -189,6 +258,20 @@
             halo(send, recv, ssem, rsem, True).wait_recv()
 
     start_halo(fh_send, fh_recv, fh_ssem, fh_rsem)
+
+    for i in range(xs):
+        p1a(i).wait_recv()
+
+        def add_pair(j, carry):
+            at_row = pl.multiple_of(j * 32, 32)
+            own = flat_b[pl.ds(pl.multiple_of((i * 2 + core) * block_rows + at_row, 32), 32), :].astype(f32)
+            total = own + p1a_recv[i, pl.ds(at_row, 32), :].astype(f32)
+            pair_sum[i, pl.ds(at_row, 32), :] = total.astype(bf16)
+            return carry
+
+        lax.fori_loop(0, block_rows // 32, add_pair, 0)
+    for d in range(1, xs):
+        p1b(d).start()
 
     for i in (13, 14, 15):
         copies[i].wait()
@@ -223,48 +306,6 @@
             ws_y(d).start()
         for d in range(1, zs):
             ws_z(d).start()
-
-    copies[4].wait()
-    first, last = CONV_ROWS // 16, flat_b.shape[0] // 16 - 1
-    flat_b[0 : 16 * first, :] = jnp.zeros((16 * first, LANES), bf16)
-    lane16 = iota((16, LANES), 1)
-
-    def moved(here, later):
-        return pltpu.roll(jnp.where(lane16 >= LANES - CONV_LANES, here, later), CONV_LANES, 1).astype(bf16)
-
-    def rest_rows(at_row, count):
-        start = at_row * LANES
-        if not isinstance(start, int):
-            start = pl.multiple_of(start, LANES)
-        return rest_v[0:1, pl.ds(start, count * LANES)].reshape(count, LANES)
-
-    def align(j, carry):
-        at_row = j * 16 - CONV_ROWS - 1
-        flat_b[pl.ds(pl.multiple_of(j * 16, 16), 16), :] = moved(rest_rows(at_row, 16), rest_rows(at_row + 1, 16))
-        return carry
-
-    lead = CONV_ROWS - 16 * first
-    start_rows = rest_rows(0, 8)
-    flat_b[16 * first : 16 * first + 16, :] = moved(
-        jnp.concatenate([jnp.zeros((lead + 1, LANES), f32), start_rows[0 : 15 - lead]], axis=0),
-        jnp.concatenate([jnp.zeros((lead, LANES), f32), start_rows[0 : 16 - lead]], axis=0),
-    )
-    lax.fori_loop(first + 1, last, align, 0)
-    end_row = 16 * last - CONV_ROWS - 1
-    end = rest_v[0:1, (end_row + 16) * LANES :]
-    end = jnp.concatenate([end, jnp.zeros((1, LANES - end.shape[1]), f32)], axis=1)
-    end_rows = rest_rows(end_row, 16)
-    flat_b[16 * last : 16 * last + 16, :] = moved(end_rows, jnp.concatenate([end_rows[1:16], end], axis=0))
-
-    def p1(d):
-        other = (s + d) % ss
-        return remote(
-            flat_b.at[pl.ds(pl.multiple_of(other * block_rows, 16), block_rows)],
-            p1_recv.at[d - 1], p1_ssem.at[d - 1], p1_rsem.at[d - 1], at(z, y, other),
-        )
-
-    for d in range(1, ss):
-        p1(d).start()
 
     row = iota((rows, 256), 0)
     lane = iota((rows, 256), 1)
@@ -347,10 +388,13 @@
         part = weights_v.at[pl.ds(pl.multiple_of(s * block_rows + owner * shard_rows, 16), shard_rows)]
         return remote(part, part, b2_ssem.at[d - 1], b2_rsem.at[d - 1], at(z, (y + d) % ys, s))
 
-    def b3(d, back):
-        owner = (s + ss - d) % ss if back else s
-        part = weights_v.at[pl.ds(pl.multiple_of(owner * block_rows, 16), block_rows)]
-        return remote(part, part, b3_ssem.at[d - 1], b3_rsem.at[d - 1], at(z, y, (s + d) % ss))
+    def b3x(d, back):
+        part = block(weights_v, (x + xs - d) % xs if back else x, core)
+        return remote(part, part, b3x_ssem.at[d - 1], b3x_rsem.at[d - 1], at(z, y, (x + d) % xs * 2 + core))
+
+    def b3c(d, back):
+        part = block(weights_v, (x + xs - d) % xs, 1 - core if back else core)
+        return remote(part, part, b3c_ssem.at[d], b3c_rsem.at[d], at(z, y, x * 2 + 1 - core))
 
     def w1(d):
         part = win_send.at[pl.ds(pl.multiple_of((s + d) % ss * win_part, 16), win_part)]
@@ -375,16 +419,20 @@
         part = win_grad.at[s % per_shard]
         return remote(part, part, wshare_ssem.at[d - 1], wshare_rsem.at[s % per_shard], at(z, y, (s + d) % ss))
 
+    def wshare_in(i):
+        part = win_grad.at[i]
+        return remote(part, part, wshare_ssem.at[0], wshare_rsem.at[i], at(z, y, (s + 1) % ss))
+
     def updated(grad, state):
         count = grad.shape[0]
         return adam_update(grad, state[0:count, :], state[count : 2 * count, :], state[2 * count : 3 * count, :])
 
     def start_ys():
-        for d in range(1, ss):
-            p1(d).wait_recv()
-        total = flat_b[pl.ds(pl.multiple_of(s * block_rows, 16), block_rows), :].astype(f32)
-        for d in range(1, ss):
-            total = total + p1_recv[d - 1].astype(f32)
+        for d in range(1, xs):
+            p1b(d).wait_recv()
+        total = pair_sum[x].astype(f32)
+        for d in range(1, xs):
+            total = total + p1b_recv[d - 1].astype(f32)
         sum_v[...] = total
         p2_send[...] = total.astype(bf16)
         for d in range(1, ys):
@@ -425,8 +473,9 @@
     def start_gather_slabs():
         for d in range(1, ys):
             b2(d, True).wait_recv()
-        for d in range(1, ss):
-            b3(d, False).start()
+        for d in range(1, xs):
+            b3x(d, False).start()
+        b3c(0, False).start()
 
     def start_window_ys():
         for d in range(1, ss):
@@ -485,8 +534,7 @@
             for i in range(per_shard):
                 @pl.when(s != y * per_shard + i)
                 def _():
-                    part = win_grad.at[i]
-                    remote(part, part, wshare_ssem.at[0], wshare_rsem.at[i], at(z, y, (s + 1) % ss)).wait_recv()
+                    wshare_in(i).wait_recv()
 
                 own_grad[i * win_part : (i + 1) * win_part, :] = win_grad[i]
 
@@ -503,7 +551,6 @@
     mask = [mask[:, :LANES], mask[:, LANES:]]
     for a in range(3):
         grad_v[a] = dot_nt(dpre_v[:, LANES : LANES + cells], feat_v[:, LANES * a : LANES * a + cells])
-    start_ys()
     for i in range(9, 13):
         copies[i].wait()
 
@@ -559,13 +606,12 @@
     for d in range(1, ss):
         w1(d).start()
 
+    start_ys()
     @pl.when((z == 0) & (y != win_y))
     def _():
         ws_y(1).wait_recv()
         for d in range(1, zs):
             ws_z(d).start()
-
-    start_zs()
 
     wait_halo(dh_send, dh_recv, dh_ssem, dh_rsem)
     spread_dpre(dh_recv[0].astype(f32), 0)
@@ -580,31 +626,42 @@
     outs[0].start()
 
     start_window_ys()
+    start_zs()
+
+    start_window_zs()
     start_gather_ys()
-    start_window_zs()
-    start_gather_slabs()
     @pl.when(z != 0)
     def _():
         ws_z(1).wait_recv()
 
     start_window_gather()
+    start_gather_slabs()
     own_update()
     for out in outs[1:4]:
         out.start()
     finish_window()
-    for d in range(1, ss):
-        b3(d, True).wait_recv()
-    for d in range(1, ss):
-        b3(d, False).wait_send()
+    nearest = sorted(range(1, xs), key=lambda d: min(d, xs - d))
+    for d in nearest:
+        b3x(d, True).wait_recv()
+        b3c(d, False).start()
+    for d in [0] + nearest:
+        b3c(d, True).wait_recv()
+    for d in range(xs):
+        b3c(d, False).wait_send()
+    for d in range(1, xs):
+        b3x(d, False).wait_send()
     for d in range(1, ys):
         b2(d, False).wait_send()
     weights_v[0:WIN, :] = win_weights[...]
     outs[4].start()
 
     for d in range(1, ss):
-        p1(d).wait_send()
         w1(d).wait_send()
         wb(d, False).wait_send()
+    for i in range(xs):
+        p1a(i).wait_send()
+    for d in range(1, xs):
+        p1b(d).wait_send()
     for d in range(1, ys):
         p2(d).wait_send()
         wy(d, False).wait_send()
@@ -710,7 +767,9 @@
             pltpu.VMEM((2, rows, LANES), bf16),
             pltpu.VMEM((2, rows, LANES), bf16),
             pltpu.VMEM((2, rows, LANES), bf16),
-            pltpu.VMEM((ss - 1, block_rows, LANES), bf16),
+            pltpu.VMEM((ss // 2, block_rows, LANES), bf16),
+            pltpu.VMEM((ss // 2, block_rows, LANES), bf16),
+            pltpu.VMEM((max(ss // 2 - 1, 1), block_rows, LANES), bf16),
             pltpu.VMEM((block_rows, LANES), f32),
             pltpu.VMEM((block_rows, LANES), bf16),
             pltpu.VMEM((ys - 1, shard_rows, LANES), bf16),
@@ -727,13 +786,15 @@
             pltpu.VMEM((WIN, LANES), bf16),
             dma((16,)), dma((5,)),
             dma((2,)), dma((2,)), dma((2,)), dma((2,)),
-            dma((ss - 1,)), dma((ss - 1,)),
+            dma((ss // 2,)), dma((ss // 2,)),
+            dma((max(ss // 2 - 1, 1),)), dma((max(ss // 2 - 1, 1),)),
             dma((ys - 1,)), dma((ys - 1,)),
             dma((zs - 1,)), dma((zs - 1,)),
             dma((zs - 1,)), dma,
             dma((ss - 1,)), dma,
             dma((ys - 1,)), dma((ys - 1,)),
-            dma((ss - 1,)), dma((ss - 1,)),
+            dma((max(ss // 2 - 1, 1),)), dma((max(ss // 2 - 1, 1),)),
+            dma((ss // 2,)), dma((ss // 2,)),
             dma((ss - 1,)), dma((ss - 1,)),
             dma((ys - 1,)), dma((ys - 1,)),
             dma((zs - 1,)), dma((zs - 1,)),

time: 58.3 us -> 47.9 us (0.82)
  Pallas kernels: 57 us -> 47.2 us
    pallas_call x1, Pallas kernels: 54.9 us -> 45.1 us  [on_device(): pl.pallas_call(functools.partial(kernel, sizes), out_shape=(jax.ShapeDtyp...]
where the time goes in v2:
time: 47.9 us; the launch traced here: 47.8 us
  Pallas kernels  47.2 us (99%)
  between operations  0.64 us (1%)
    pallas_call x1, Pallas kernels, on_device(): pl.pallas_call(functools.partial(kernel, sizes), out_shape=(jax.ShapeDtyp...  45.1 us
    pallas_call x1, Pallas kernels, on_device(): pl.pallas_call(copy_kernel, out_shape=tuple((jax.ShapeDtypeStruct(out.sha...  2.08 us

profile of v2, /device:TPU:1, one launch (start us, length us, event | category | flops | bytes accessed | tf_op | source)
XLA Modules:
  0.0 47.8 jit_solution(11690820725555013773)
XLA Ops:
  0.6 45.1 %shard_map.191 = (bf16[24,4,8,128]{3,2,1,0:T(8,128)(2,1)}, f32[32,128]{1,0:T(8,128)}, f32[32,128]{1,0:T(8,128)}, f32[32,128]{1,0:T(8,128)}, bf16[2048,128]{1,0:T(8,128)(2,1)}) custom-call(bf16[24,4,8,128]{3,2,1,0:T(8,128)(2,1)} %bitcast.15, bf16[16,4,8,128]{3,2,1,0:T(8,128)(2,1)} %bitcast.17, bf16[27,24,24]{2,1,0:T(8,128)(2,1)} %bitcast.16, ...), custom_call_target="tpu_custom_call" | custom-call | tf_op jit(solution)/shard_map/pallas_call | solution.py:732
  45.7 2.1 %shard_map.192 = (bf16[24,4,8,128]{3,2,1,0:T(8,128)(2,1)}, f32[32,128]{1,0:T(8,128)}, f32[32,128]{1,0:T(8,128)}, f32[32,128]{1,0:T(8,128)}, bf16[2048,128]{1,0:T(8,128)(2,1)}) custom-call(bf16[24,4,8,128]{3,2,1,0:T(8,128)(2,1)} %get-tuple-element.15.refs_0_, f32[32,128]{1,0:T(8,128)} %get-tuple-element.16.refs_1_, f32[32,128]{1,0:T(8,128)} %get-tuple-element.17.refs_2_, ...), custom_call_target="tpu_custom_call" | custom-call | tf_op jit(solution)/shard_map/pallas_call | solution.py:820

commit v3 on v2

--- a/solution.py
+++ b/solution.py
@@ -72,6 +72,10 @@
     return tuple(jnp.asarray(t, bf16) for t in tables)
 
 
+def far_first(count):
+    return sorted(range(1, count), key=lambda d: -min(d, count - d))
+
+
 def dot(lhs, rhs):
     return jnp.dot(lhs, rhs, preferred_element_type=f32)
 
@@ -124,12 +128,13 @@
         )
 
     barrier = pltpu.get_barrier_semaphore()
-    for d in range(1, ss):
-        pl.semaphore_signal(barrier, inc=1, device_id=at(z, y, (s + d) % ss), device_id_type=MESH)
-    for d in range(1, ys):
-        pl.semaphore_signal(barrier, inc=1, device_id=at(z, (y + d) % ys, s), device_id_type=MESH)
-    for d in range(1, zs):
-        pl.semaphore_signal(barrier, inc=1, device_id=at((z + d) % zs, y, s), device_id_type=MESH)
+    for d in far_first(max(ys, zs, ss)):
+        if d < zs:
+            pl.semaphore_signal(barrier, inc=1, device_id=at((z + d) % zs, y, s), device_id_type=MESH)
+        if d < ys:
+            pl.semaphore_signal(barrier, inc=1, device_id=at(z, (y + d) % ys, s), device_id_type=MESH)
+        if d < ss:
+            pl.semaphore_signal(barrier, inc=1, device_id=at(z, y, (s + d) % ss), device_id_type=MESH)
 
     ins = (
         (feat_in, feat_ref), (w_in, w_ref), (rep_lanes_in, rep_lanes_ref), (rep_rows_in, rep_rows_ref),
@@ -190,6 +195,30 @@
     end_rows = rest_rows(end_row * LANES, 16)
     flat_b[16 * last : 16 * last + 16, :] = moved(end_rows, jnp.concatenate([end_rows[1:16], end], axis=0))
 
+    pl.semaphore_wait(barrier, (ss - 1) + (ys - 1) + (zs - 1))
+
+    xs = ss // 2
+    x = s // 2
+    core = s % 2
+
+    def block(ref, xx, cc):
+        return ref.at[pl.ds(pl.multiple_of((xx * 2 + cc) * block_rows, 16), block_rows)]
+
+    def p1a(i):
+        return remote(
+            block(flat_b, i, 1 - core), p1a_recv.at[i], p1a_ssem.at[i], p1a_rsem.at[i], at(z, y, x * 2 + 1 - core)
+        )
+
+    def p1b(d):
+        to = (x + d) % xs
+        return remote(
+            pair_sum.at[to], p1b_recv.at[d - 1], p1b_ssem.at[d - 1], p1b_rsem.at[d - 1], at(z, y, to * 2 + core)
+        )
+
+    order = [(x + d) % xs for d in far_first(xs) + [0]]
+    for i in order:
+        p1a(i).start()
+
     copies[0].wait()
     for p in range(planes):
         plane = feat_ref[:, p].astype(f32).reshape(rows, LANES).astype(bf16)
@@ -201,29 +230,6 @@
     feat_v[rows : rows + 16, :] = jnp.ones((16, cells + 2 * LANES), bf16)
     feat_v[rows + 16 : 256, :] = jnp.zeros((256 - rows - 16, cells + 2 * LANES), bf16)
 
-    pl.semaphore_wait(barrier, (ss - 1) + (ys - 1) + (zs - 1))
-
-    xs = ss // 2
-    x = s // 2
-    core = s % 2
-
-    def block(ref, xx, cc):
-        return ref.at[pl.ds(pl.multiple_of((xx * 2 + cc) * block_rows, 16), block_rows)]
-
-    def p1a(i):
-        return remote(
-            block(flat_b, i, 1 - core), p1a_recv.at[i], p1a_ssem.at[i], p1a_rsem.at[i], at(z, y, x * 2 + 1 - core)
-        )
-
-    def p1b(d):
-        to = (x + d) % xs
-        return remote(
-            pair_sum.at[to], p1b_recv.at[d - 1], p1b_ssem.at[d - 1], p1b_rsem.at[d - 1], at(z, y, to * 2 + core)
-        )
-
-    for i in range(xs):
-        p1a(i).start()
-
     def halo(send, recv, ssem, rsem, up):
         source, slot = (1, 0) if up else (0, 1)
         other = (s + 1) % ss if up else (s + ss - 1) % ss
@@ -259,19 +265,13 @@
 
     start_halo(fh_send, fh_recv, fh_ssem, fh_rsem)
 
-    for i in range(xs):
-        p1a(i).wait_recv()
-
-        def add_pair(j, carry):
-            at_row = pl.multiple_of(j * 32, 32)
-            own = flat_b[pl.ds(pl.multiple_of((i * 2 + core) * block_rows + at_row, 32), 32), :].astype(f32)
-            total = own + p1a_recv[i, pl.ds(at_row, 32), :].astype(f32)
-            pair_sum[i, pl.ds(at_row, 32), :] = total.astype(bf16)
-            return carry
-
-        lax.fori_loop(0, block_rows // 32, add_pair, 0)
-    for d in range(1, xs):
-        p1b(d).start()
+    for d in far_first(xs) + [0]:
+        to = (x + d) % xs
+        p1a(to).wait_recv()
+        own = flat_b[pl.ds(pl.multiple_of((to * 2 + core) * block_rows, 16), block_rows), :].astype(f32)
+        pair_sum[to] = (own + p1a_recv[to].astype(f32)).astype(bf16)
+        if d:
+            p1b(d).start()
 
     for i in (13, 14, 15):
         copies[i].wait()
@@ -292,7 +292,7 @@
 
     @pl.when(reducer)
     def _():
-        for d in range(1, zs):
+        for d in far_first(zs):
             col(d).start()
         col_state[...] = own_state[...]
 
@@ -302,9 +302,9 @@
             win_state[i * win_part : (i + 1) * win_part, :] = own_state[
                 pl.ds(pl.multiple_of(i * shard_rows + win_row, 16), win_part), :
             ]
-        for d in range(1, ys):
+        for d in far_first(ys):
             ws_y(d).start()
-        for d in range(1, zs):
+        for d in far_first(zs):
             ws_z(d).start()
 
     row = iota((rows, 256), 0)
@@ -435,7 +435,7 @@
             total = total + p1b_recv[d - 1].astype(f32)
         sum_v[...] = total
         p2_send[...] = total.astype(bf16)
-        for d in range(1, ys):
+        for d in far_first(ys):
             p2(d).start()
 
     def start_zs():
@@ -445,7 +445,7 @@
         for d in range(1, ys):
             total = total + p2_recv[d - 1].astype(f32)
         p3_all[z] = total.astype(bf16)
-        for d in range(1, zs):
+        for d in far_first(zs):
             p3(d, False).start()
 
     def start_gather_ys():
@@ -461,7 +461,7 @@
         grad = grad / LOSS_SCALE
         weights = updated(grad, col_state)[2].astype(bf16)
         weights_v[pl.ds(pl.multiple_of(s * block_rows + y * shard_rows, 16), shard_rows), :] = weights
-        for d in range(1, ys):
+        for d in far_first(ys):
             b2(d, False).start()
 
         @pl.when(reducer)
@@ -473,7 +473,7 @@
     def start_gather_slabs():
         for d in range(1, ys):
             b2(d, True).wait_recv()
-        for d in range(1, xs):
+        for d in far_first(xs):
             b3x(d, False).start()
         b3c(0, False).start()
 
@@ -484,7 +484,7 @@
         for d in range(1, ss):
             total = total + win_recv[d - 1].astype(f32)
         wy_all[y] = total.astype(bf16)
-        for d in range(1, ys):
+        for d in far_first(ys):
             wy(d, False).start()
 
     def start_window_zs():
@@ -494,7 +494,7 @@
         for i in range(1, ys):
             total = total + wy_all[i].astype(f32)
         wz_all[z] = total.astype(bf16)
-        for d in range(1, zs):
+        for d in far_first(zs):
             wz(d, False).start()
 
     in_window = (z == 0) & (y < WIN // shard_rows)
@@ -545,7 +545,6 @@
     outs += [
         pltpu.make_async_copy(shards_v.at[i], ref, out_sem.at[1 + i]) for i, ref in enumerate((nmom_out, nsec_out, nmas_out))
     ]
-    outs += [pltpu.make_async_copy(weights_v, weights_out, out_sem.at[4])]
 
     mask = ((lane < rows) & (shift >= -1) & (shift <= 1)) | ((lane >= rows) & (lane < rows + 8) & (shift == 0))
     mask = [mask[:, :LANES], mask[:, LANES:]]
@@ -610,7 +609,7 @@
     @pl.when((z == 0) & (y != win_y))
     def _():
         ws_y(1).wait_recv()
-        for d in range(1, zs):
+        for d in far_first(zs):
             ws_z(d).start()
 
     wait_halo(dh_send, dh_recv, dh_ssem, dh_rsem)
@@ -640,12 +639,23 @@
     for out in outs[1:4]:
         out.start()
     finish_window()
+    def out_block(xx, cc, sem):
+        return pltpu.make_async_copy(block(weights_v, xx, cc), block(weights_out, xx, cc), out_sem.at[4 + sem])
+
+    def write_block(xx, cc, sem):
+        @pl.when((xx > 0) | (cc > 0))
+        def _():
+            out_block(xx, cc, sem).start()
+
+    write_block(x, core, 0)
     nearest = sorted(range(1, xs), key=lambda d: min(d, xs - d))
     for d in nearest:
         b3x(d, True).wait_recv()
         b3c(d, False).start()
+        write_block((x + xs - d) % xs, core, d)
     for d in [0] + nearest:
         b3c(d, True).wait_recv()
+        write_block((x + xs - d) % xs, 1 - core, xs + d)
     for d in range(xs):
         b3c(d, False).wait_send()
     for d in range(1, xs):
@@ -653,7 +663,11 @@
     for d in range(1, ys):
         b2(d, False).wait_send()
     weights_v[0:WIN, :] = win_weights[...]
-    outs[4].start()
+    for d in range(xs):
+        for cc in range(2):
+            @pl.when(((x + xs - d) % xs == 0) & ((core if cc == 0 else 1 - core) == 0))
+            def _():
+                out_block(0, 0, cc * xs + d).start()
 
     for d in range(1, ss):
         w1(d).wait_send()
@@ -693,13 +707,19 @@
 
     for out in outs:
         out.wait()
+    for d in range(xs):
+        for cc in range(2):
+            out_block((x + xs - d) % xs, core if cc == 0 else 1 - core, cc * xs + d).wait()
 
 
 def copy_kernel(*refs):
     count = (len(refs) - 2) // 3
     in_sem, out_sem = refs[3 * count :]
-    loads = [pltpu.make_async_copy(refs[i], refs[2 * count + i], in_sem.at[i]) for i in range(count)]
-    stores = [pltpu.make_async_copy(refs[2 * count + i], refs[count + i], out_sem.at[i]) for i in range(count)]
+    ins, outs, held = refs[:count], refs[count : 2 * count], refs[2 * count : 3 * count]
+    part = ins[-1].shape[0] // 4
+    pieces = [(i, slice(None)) for i in range(count - 1)] + [(count - 1, pl.ds(part * j, part)) for j in range(4)]
+    loads = [pltpu.make_async_copy(ins[i].at[p], held[i].at[p], in_sem.at[k]) for k, (i, p) in enumerate(pieces)]
+    stores = [pltpu.make_async_copy(held[i].at[p], outs[i].at[p], out_sem.at[k]) for k, (i, p) in enumerate(pieces)]
     for load in loads:
         load.start()
     for load, store in zip(loads, stores):
@@ -784,7 +804,7 @@
             pltpu.VMEM((3 * win_part, LANES), f32),
             pltpu.VMEM((shard_rows // win_part, win_part, LANES), f32),
             pltpu.VMEM((WIN, LANES), bf16),
-            dma((16,)), dma((5,)),
+            dma((16,)), dma((4 + ss,)),
             dma((2,)), dma((2,)), dma((2,)), dma((2,)),
             dma((ss // 2,)), dma((ss // 2,)),
             dma((max(ss // 2 - 1, 1),)), dma((max(ss // 2 - 1, 1),)),
@@ -822,7 +842,7 @@
         out_shape=tuple(jax.ShapeDtypeStruct(out.shape, out.dtype) for out in outs),
         in_specs=[pl.BlockSpec(memory_space=pl.ANY)] * 5,
         out_specs=(pl.BlockSpec(memory_space=pl.ANY),) * 5,
-        scratch_shapes=[pltpu.VMEM(out.shape, out.dtype) for out in outs] + [dma((5,)), dma((5,))],
+        scratch_shapes=[pltpu.VMEM(out.shape, out.dtype) for out in outs] + [dma((8,)), dma((8,))],
         compiler_params=pltpu.CompilerParams(vmem_limit_bytes=60 << 20),
     )(*outs)
     return (

time: 47.9 us -> 46.8 us (0.977)
  Pallas kernels: 47.2 us -> 46 us
    pallas_call x1, Pallas kernels: 45.1 us -> 43.9 us  [on_device(): pl.pallas_call(functools.partial(kernel, sizes), out_shape=(jax.ShapeDtyp...]
where the time goes in v3:
time: 46.8 us; the launch traced here: 46.6 us
  Pallas kernels  46 us (98%)
  between operations  0.64 us (1%)
    pallas_call x1, Pallas kernels, on_device(): pl.pallas_call(functools.partial(kernel, sizes), out_shape=(jax.ShapeDtyp...  43.9 us
    pallas_call x1, Pallas kernels, on_device(): pl.pallas_call(copy_kernel, out_shape=tuple((jax.ShapeDtypeStruct(out.sha...  2.05 us

profile of v3, /device:TPU:1, one launch (start us, length us, event | category | flops | bytes accessed | tf_op | source)
XLA Modules:
  0.0 46.6 jit_solution(18071381997352101393)
XLA Ops:
  0.6 43.9 %shard_map.191 = (bf16[24,4,8,128]{3,2,1,0:T(8,128)(2,1)}, f32[32,128]{1,0:T(8,128)}, f32[32,128]{1,0:T(8,128)}, f32[32,128]{1,0:T(8,128)}, bf16[2048,128]{1,0:T(8,128)(2,1)}) custom-call(bf16[24,4,8,128]{3,2,1,0:T(8,128)(2,1)} %bitcast.15, bf16[16,4,8,128]{3,2,1,0:T(8,128)(2,1)} %bitcast.17, bf16[27,24,24]{2,1,0:T(8,128)(2,1)} %bitcast.16, ...), custom_call_target="tpu_custom_call" | custom-call | tf_op jit(solution)/shard_map/pallas_call | solution.py:752
  44.6 2.0 %shard_map.192 = (bf16[24,4,8,128]{3,2,1,0:T(8,128)(2,1)}, f32[32,128]{1,0:T(8,128)}, f32[32,128]{1,0:T(8,128)}, f32[32,128]{1,0:T(8,128)}, bf16[2048,128]{1,0:T(8,128)(2,1)}) custom-call(bf16[24,4,8,128]{3,2,1,0:T(8,128)(2,1)} %get-tuple-element.15.refs_0_, f32[32,128]{1,0:T(8,128)} %get-tuple-element.16.refs_1_, f32[32,128]{1,0:T(8,128)} %get-tuple-element.17.refs_2_, ...), custom_call_target="tpu_custom_call" | custom-call | tf_op jit(solution)/shard_map/pallas_call | solution.py:840

commit v4 on v3

--- a/solution.py
+++ b/solution.py
@@ -99,7 +99,7 @@
     igrad_out, nmom_out, nsec_out, nmas_out, weights_out,
     feat_ref, cot_ref, w_ref, bias_ref, headt_ref, rest_1d, own_state,
     rep_rows_ref, rep_lanes_ref, rep_emb_ref, add_ref, order_ref, emb_order_ref, place_ref,
-    igrad_v, shards_v, weights_v,
+    igrad_v, shards_v, weights_v, ordered_v,
     flat_b, feat_v, cot_v, wband, hband, conv_v, act_v, dpre_v, grad_v, packed_v, stack_v,
     fh_send, fh_recv, dh_send, dh_recv,
     p1a_recv, pair_sum, p1b_recv, sum_v, p2_send, p2_recv, p3_all, col_state, grad_shard, own_grad,
@@ -383,18 +383,30 @@
     def share(d):
         return remote(grad_shard, grad_shard, share_ssem.at[d - 1], share_rsem, at(z, y, (s + d) % ss))
 
-    def b2(d, back):
-        owner = (y + ys - d) % ys if back else y
-        part = weights_v.at[pl.ds(pl.multiple_of(s * block_rows + owner * shard_rows, 16), shard_rows)]
-        return remote(part, part, b2_ssem.at[d - 1], b2_rsem.at[d - 1], at(z, (y + d) % ys, s))
-
-    def b3x(d, back):
-        part = block(weights_v, (x + xs - d) % xs if back else x, core)
-        return remote(part, part, b3x_ssem.at[d - 1], b3x_rsem.at[d - 1], at(z, y, (x + d) % xs * 2 + core))
+    near = ys // 4
+    near_count = 2 * near + 1
+
+    def shards_of(xx, slot, count):
+        at_row = (xx * 2 + core) * block_rows + slot * shard_rows
+        return weights_v.at[pl.ds(pl.multiple_of(at_row, 16), count * shard_rows)]
+
+    def b2(d):
+        return remote(
+            shards_of(x, near, 1), shards_of(x, (near - d) % ys, 1),
+            b2_ssem.at[d - 1], b2_rsem.at[d - 1], at(z, (y + d) % ys, s),
+        )
+
+    def b3x(d, far, back):
+        slot, count = (near_count, ys - near_count) if far else (0, near_count)
+        part = shards_of((x + xs - d) % xs if back else x, slot, count)
+        return remote(part, part, b3x_ssem.at[d - 1, far], b3x_rsem.at[d - 1, far], at(z, y, (x + d) % xs * 2 + core))
 
     def b3c(d, back):
-        part = block(weights_v, (x + xs - d) % xs, 1 - core if back else core)
-        return remote(part, part, b3c_ssem.at[d], b3c_rsem.at[d], at(z, y, x * 2 + 1 - core))
+        xx = (x + xs - d) % xs
+        return remote(
+            block(ordered_v, xx, core), block(weights_out, xx, 1 - core if back else core),
+            b3c_ssem.at[d], b3c_rsem.at[d], at(z, y, x * 2 + 1 - core),
+        )
 
     def w1(d):
         part = win_send.at[pl.ds(pl.multiple_of((s + d) % ss * win_part, 16), win_part)]
@@ -460,9 +472,9 @@
             grad = grad + p3_all[i].astype(f32)
         grad = grad / LOSS_SCALE
         weights = updated(grad, col_state)[2].astype(bf16)
-        weights_v[pl.ds(pl.multiple_of(s * block_rows + y * shard_rows, 16), shard_rows), :] = weights
+        weights_v[pl.ds(pl.multiple_of(s * block_rows + near * shard_rows, 16), shard_rows), :] = weights
         for d in far_first(ys):
-            b2(d, False).start()
+            b2(d).start()
 
         @pl.when(reducer)
         def _():
@@ -471,11 +483,12 @@
                 share(d).start()
 
     def start_gather_slabs():
-        for d in range(1, ys):
-            b2(d, True).wait_recv()
-        for d in far_first(xs):
-            b3x(d, False).start()
-        b3c(0, False).start()
+        for far in range(2):
+            for d in range(1, ys):
+                if (min(d, ys - d) > near) == bool(far):
+                    b2(d).wait_recv()
+            for d in far_first(xs):
+                b3x(d, far, False).start()
 
     def start_window_ys():
         for d in range(1, ss):
@@ -635,39 +648,38 @@
 
     start_window_gather()
     start_gather_slabs()
+    finish_window()
+
+    def out_block(d):
+        xx = (x + xs - d) % xs
+        return pltpu.make_async_copy(block(ordered_v, xx, core), block(weights_out, xx, core), out_sem.at[4 + d])
+
+    def finish_block(d):
+        xx = (x + xs - d) % xs
+        base = (xx * 2 + core) * block_rows
+        for slot in range(ys):
+            owner = (y + ys + slot - near) % ys
+            ordered_v[pl.ds(pl.multiple_of(base + owner * shard_rows, 16), shard_rows), :] = weights_v[
+                pl.ds(pl.multiple_of(base + slot * shard_rows, 16), shard_rows), :
+            ]
+
+        @pl.when((xx == 0) & (core == 0))
+        def _():
+            ordered_v[0:WIN, :] = win_weights[...]
+
+        b3c(d, False).start()
+        out_block(d).start()
+
+    finish_block(0)
     own_update()
     for out in outs[1:4]:
         out.start()
-    finish_window()
-    def out_block(xx, cc, sem):
-        return pltpu.make_async_copy(block(weights_v, xx, cc), block(weights_out, xx, cc), out_sem.at[4 + sem])
-
-    def write_block(xx, cc, sem):
-        @pl.when((xx > 0) | (cc > 0))
-        def _():
-            out_block(xx, cc, sem).start()
-
-    write_block(x, core, 0)
-    nearest = sorted(range(1, xs), key=lambda d: min(d, xs - d))
-    for d in nearest:
-        b3x(d, True).wait_recv()
-        b3c(d, False).start()
-        write_block((x + xs - d) % xs, core, d)
-    for d in [0] + nearest:
+    for d in sorted(range(1, xs), key=lambda d: min(d, xs - d)):
+        for far in range(2):
+            b3x(d, far, True).wait_recv()
+        finish_block(d)
+    for d in range(xs):
         b3c(d, True).wait_recv()
-        write_block((x + xs - d) % xs, 1 - core, xs + d)
-    for d in range(xs):
-        b3c(d, False).wait_send()
-    for d in range(1, xs):
-        b3x(d, False).wait_send()
-    for d in range(1, ys):
-        b2(d, False).wait_send()
-    weights_v[0:WIN, :] = win_weights[...]
-    for d in range(xs):
-        for cc in range(2):
-            @pl.when(((x + xs - d) % xs == 0) & ((core if cc == 0 else 1 - core) == 0))
-            def _():
-                out_block(0, 0, cc * xs + d).start()
 
     for d in range(1, ss):
         w1(d).wait_send()
@@ -705,11 +717,16 @@
         for d in range(1, ss):
             wshare(d).wait_send()
 
+    for d in range(xs):
+        b3c(d, False).wait_send()
+        out_block(d).wait()
+    for d in range(1, xs):
+        for far in range(2):
+            b3x(d, far, False).wait_send()
+    for d in range(1, ys):
+        b2(d).wait_send()
     for out in outs:
         out.wait()
-    for d in range(xs):
-        for cc in range(2):
-            out_block((x + xs - d) % xs, core if cc == 0 else 1 - core, cc * xs + d).wait()
 
 
 def copy_kernel(*refs):
@@ -773,6 +790,7 @@
             pltpu.VMEM((3, shard_rows, LANES), f32),
             pltpu.VMEM((all_rows, LANES), bf16),
             pltpu.VMEM((all_rows, LANES), bf16),
+            pltpu.VMEM((all_rows, LANES), bf16),
             pltpu.VMEM((256, cells + 2 * LANES), bf16),
             pltpu.VMEM((8 * emb, cells), bf16),
             pltpu.VMEM((3, 3 * rows, 256), bf16),
@@ -813,7 +831,7 @@
             dma((zs - 1,)), dma,
             dma((ss - 1,)), dma,
             dma((ys - 1,)), dma((ys - 1,)),
-            dma((max(ss // 2 - 1, 1),)), dma((max(ss // 2 - 1, 1),)),
+            dma((max(ss // 2 - 1, 1), 2)), dma((max(ss // 2 - 1, 1), 2)),
             dma((ss // 2,)), dma((ss // 2,)),
             dma((ss - 1,)), dma((ss - 1,)),
             dma((ys - 1,)), dma((ys - 1,)),

time: 46.8 us -> 46 us (0.983)
  Pallas kernels: 46 us -> 45.2 us
    pallas_call x1, Pallas kernels: 43.9 us -> 43.2 us  [on_device(): pl.pallas_call(functools.partial(kernel, sizes), out_shape=(jax.ShapeDtyp...]
where the time goes in v4:
time: 46 us; the launch traced here: 45.9 us
  Pallas kernels  45.2 us (98%)
  between operations  0.64 us (1%)
    pallas_call x1, Pallas kernels, on_device(): pl.pallas_call(functools.partial(kernel, sizes), out_shape=(jax.ShapeDtyp...  43.2 us
    pallas_call x1, Pallas kernels, on_device(): pl.pallas_call(copy_kernel, out_shape=tuple((jax.ShapeDtypeStruct(out.sha...  2.05 us

profile of v4, /device:TPU:1, one launch (start us, length us, event | category | flops | bytes accessed | tf_op | source)
XLA Modules:
  0.0 45.9 jit_solution(648228918037040168)
XLA Ops:
  0.6 43.2 %shard_map.191 = (bf16[24,4,8,128]{3,2,1,0:T(8,128)(2,1)}, f32[32,128]{1,0:T(8,128)}, f32[32,128]{1,0:T(8,128)}, f32[32,128]{1,0:T(8,128)}, bf16[2048,128]{1,0:T(8,128)(2,1)}) custom-call(bf16[24,4,8,128]{3,2,1,0:T(8,128)(2,1)} %bitcast.15, bf16[16,4,8,128]{3,2,1,0:T(8,128)(2,1)} %bitcast.17, bf16[27,24,24]{2,1,0:T(8,128)(2,1)} %bitcast.16, ...), custom_call_target="tpu_custom_call" | custom-call | tf_op jit(solution)/shard_map/pallas_call | solution.py:769
  43.8 2.0 %shard_map.192 = (bf16[24,4,8,128]{3,2,1,0:T(8,128)(2,1)}, f32[32,128]{1,0:T(8,128)}, f32[32,128]{1,0:T(8,128)}, f32[32,128]{1,0:T(8,128)}, bf16[2048,128]{1,0:T(8,128)(2,1)}) custom-call(bf16[24,4,8,128]{3,2,1,0:T(8,128)(2,1)} %get-tuple-element.15.refs_0_, f32[32,128]{1,0:T(8,128)} %get-tuple-element.16.refs_1_, f32[32,128]{1,0:T(8,128)} %get-tuple-element.17.refs_2_, ...), custom_call_target="tpu_custom_call" | custom-call | tf_op jit(solution)/shard_map/pallas_call | solution.py:858

commit v5 on v4

--- a/solution.py
+++ b/solution.py
@@ -100,7 +100,7 @@
     feat_ref, cot_ref, w_ref, bias_ref, headt_ref, rest_1d, own_state,
     rep_rows_ref, rep_lanes_ref, rep_emb_ref, add_ref, order_ref, emb_order_ref, place_ref,
     igrad_v, shards_v, weights_v, ordered_v,
-    flat_b, feat_v, cot_v, wband, hband, conv_v, act_v, dpre_v, grad_v, packed_v, stack_v,
+    shared_rows, flat_b, feat_v, cot_v, wband, hband, conv_v, act_v, dpre_v, grad_v, packed_v, stack_v,
     fh_send, fh_recv, dh_send, dh_recv,
     p1a_recv, pair_sum, p1b_recv, sum_v, p2_send, p2_recv, p3_all, col_state, grad_shard, own_grad,
     win_send, win_recv, wy_all, wz_all, win_state, win_grad, win_weights,
@@ -147,9 +147,24 @@
     for copy in copies:
         copy.start()
 
+    near = ys // 4
+    near_count = 2 * near + 1
+    far_count = ys - near_count
+    far_rows = far_count * shard_rows
+
+    def placed(row):
+        block_at = lax.div(row, block_rows)
+        in_block = lax.rem(row, block_rows)
+        slot = lax.rem(lax.div(in_block, shard_rows) + (2 * ys - near - 1) - y, ys)
+        return pl.multiple_of(block_at * block_rows + slot * shard_rows + lax.rem(in_block, shard_rows), 16)
+
+    def store_rows(row, value):
+        flat_b[pl.ds(placed(jnp.int32(row)), 16), :] = value
+
     copies[4].wait()
     first, last = CONV_ROWS // 16, flat_b.shape[0] // 16 - 1
-    flat_b[0 : 16 * first, :] = jnp.zeros((16 * first, LANES), bf16)
+    for j in range(first):
+        store_rows(16 * j, jnp.zeros((16, LANES), bf16))
     lane16 = iota((16, LANES), 1)
 
     def moved(here, later):
@@ -172,7 +187,7 @@
             start = (at_row + 8 * h) * LANES + skipped
             halves.append(moved8(rest_rows(start, 8), rest_rows(start + LANES, 8)))
         part = jnp.concatenate(halves, axis=0).astype(bf16)
-        flat_b[pl.ds(at_row + 16 * (first + 1), 16), :] = part
+        store_rows(at_row + 16 * (first + 1), part)
 
     def align(j, carry):
         for i in range(per_step):
@@ -185,15 +200,16 @@
         align_at(16 * j)
     lead = CONV_ROWS - 16 * first
     start_rows = rest_rows(0, 8)
-    flat_b[16 * first : 16 * first + 16, :] = moved(
+    shared_rows[...] = moved(
         jnp.concatenate([jnp.zeros((lead + 1, LANES), f32), start_rows[0 : 15 - lead]], axis=0),
         jnp.concatenate([jnp.zeros((lead, LANES), f32), start_rows[0 : 16 - lead]], axis=0),
     )
+    store_rows(16 * first, shared_rows[...])
     end_row = 16 * last - CONV_ROWS - 1
     end = rest_1d[0:1, (end_row + 16) * LANES :]
     end = jnp.concatenate([end, jnp.zeros((1, LANES - end.shape[1]), f32)], axis=1)
     end_rows = rest_rows(end_row * LANES, 16)
-    flat_b[16 * last : 16 * last + 16, :] = moved(end_rows, jnp.concatenate([end_rows[1:16], end], axis=0))
+    store_rows(16 * last, moved(end_rows, jnp.concatenate([end_rows[1:16], end], axis=0)))
 
     pl.semaphore_wait(barrier, (ss - 1) + (ys - 1) + (zs - 1))
 
@@ -209,10 +225,12 @@
             block(flat_b, i, 1 - core), p1a_recv.at[i], p1a_ssem.at[i], p1a_rsem.at[i], at(z, y, x * 2 + 1 - core)
         )
 
-    def p1b(d):
+    def p1b(d, part):
         to = (x + d) % xs
+        some = pl.ds(far_rows, block_rows - far_rows) if part else pl.ds(0, far_rows)
         return remote(
-            pair_sum.at[to], p1b_recv.at[d - 1], p1b_ssem.at[d - 1], p1b_rsem.at[d - 1], at(z, y, to * 2 + core)
+            pair_sum.at[to, some], p1b_recv.at[d - 1, some],
+            p1b_ssem.at[d - 1, part], p1b_rsem.at[d - 1, part], at(z, y, to * 2 + core),
         )
 
     order = [(x + d) % xs for d in far_first(xs) + [0]]
@@ -271,7 +289,9 @@
         own = flat_b[pl.ds(pl.multiple_of((to * 2 + core) * block_rows, 16), block_rows), :].astype(f32)
         pair_sum[to] = (own + p1a_recv[to].astype(f32)).astype(bf16)
         if d:
-            p1b(d).start()
+            p1b(d, 0).start()
+    for d in far_first(xs):
+        p1b(d, 1).start()
 
     for i in (13, 14, 15):
         copies[i].wait()
@@ -370,10 +390,10 @@
     act_v[rows : rows + 16, :] = jnp.ones((16, cells), bf16)
 
     def p2(d):
-        other = (y + d) % ys
+        slot = (d - near - 1) % ys
         return remote(
-            p2_send.at[pl.ds(pl.multiple_of(other * shard_rows, 16), shard_rows)],
-            p2_recv.at[d - 1], p2_ssem.at[d - 1], p2_rsem.at[d - 1], at(z, other, s),
+            p2_send.at[pl.ds(slot * shard_rows, shard_rows)], p2_recv.at[d - 1],
+            p2_ssem.at[d - 1], p2_rsem.at[d - 1], at(z, (y + d) % ys, s),
         )
 
     def p3(d, back):
@@ -382,9 +402,6 @@
 
     def share(d):
         return remote(grad_shard, grad_shard, share_ssem.at[d - 1], share_rsem, at(z, y, (s + d) % ss))
-
-    near = ys // 4
-    near_count = 2 * near + 1
 
     def shards_of(xx, slot, count):
         at_row = (xx * 2 + core) * block_rows + slot * shard_rows
@@ -440,20 +457,22 @@
         return adam_update(grad, state[0:count, :], state[count : 2 * count, :], state[2 * count : 3 * count, :])
 
     def start_ys():
-        for d in range(1, xs):
-            p1b(d).wait_recv()
-        total = pair_sum[x].astype(f32)
-        for d in range(1, xs):
-            total = total + p1b_recv[d - 1].astype(f32)
-        sum_v[...] = total
-        p2_send[...] = total.astype(bf16)
-        for d in far_first(ys):
-            p2(d).start()
+        for part, some in enumerate((slice(0, far_rows), slice(far_rows, block_rows))):
+            for d in range(1, xs):
+                p1b(d, part).wait_recv()
+            total = pair_sum[x, some].astype(f32)
+            for d in range(1, xs):
+                total = total + p1b_recv[d - 1, some].astype(f32)
+            sum_v[some, :] = total
+            p2_send[some, :] = total.astype(bf16)
+            for d in far_first(ys):
+                if (min(d, ys - d) <= near) == bool(part):
+                    p2(d).start()
 
     def start_zs():
         for d in range(1, ys):
             p2(d).wait_recv()
-        total = sum_v[pl.ds(pl.multiple_of(y * shard_rows, 16), shard_rows), :]
+        total = sum_v[(ys - 1 - near) * shard_rows : (ys - near) * shard_rows, :]
         for d in range(1, ys):
             total = total + p2_recv[d - 1].astype(f32)
         p3_all[z] = total.astype(bf16)
@@ -613,8 +632,9 @@
         piece = pltpu.roll(hgrad[8 * t : 8 * t + 8], 0, 1, stride=16, stride_axis=0)
         stack_v[192 + 8 * t : 200 + 8 * t, :] = jnp.where(lane8 >= 88, piece, 0.0)
         stack_v[224 + 8 * t : 232 + 8 * t, :] = jnp.where(lane8 < 88, piece, 0.0)
-    window = dot(place_ref[...], stack_v[...].astype(bf16)) + flat_b[0:WIN, :].astype(f32)
-    win_send[...] = window.astype(bf16)
+    window = dot(place_ref[...], stack_v[...].astype(bf16))
+    win_send[0 : 16 * first, :] = window[0 : 16 * first].astype(bf16)
+    win_send[16 * first : WIN, :] = (window[16 * first : WIN] + shared_rows[...].astype(f32)).astype(bf16)
     for d in range(1, ss):
         w1(d).start()
 
@@ -648,36 +668,43 @@
 
     start_window_gather()
     start_gather_slabs()
-    finish_window()
-
     def out_block(d):
         xx = (x + xs - d) % xs
         return pltpu.make_async_copy(block(ordered_v, xx, core), block(weights_out, xx, core), out_sem.at[4 + d])
 
     def finish_block(d):
-        xx = (x + xs - d) % xs
-        base = (xx * 2 + core) * block_rows
+        base = ((x + xs - d) % xs * 2 + core) * block_rows
         for slot in range(ys):
             owner = (y + ys + slot - near) % ys
             ordered_v[pl.ds(pl.multiple_of(base + owner * shard_rows, 16), shard_rows), :] = weights_v[
                 pl.ds(pl.multiple_of(base + slot * shard_rows, 16), shard_rows), :
             ]
 
-        @pl.when((xx == 0) & (core == 0))
-        def _():
-            ordered_v[0:WIN, :] = win_weights[...]
-
-        b3c(d, False).start()
-        out_block(d).start()
-
+        @pl.when((x != d) | (core != 0))
+        def _():
+            b3c(d, False).start()
+            out_block(d).start()
+
+    nearest = sorted(range(1, xs), key=lambda d: min(d, xs - d))
     finish_block(0)
+    for d in nearest:
+        for far in range(2):
+            b3x(d, far, True).wait_recv()
+        finish_block(d)
+    finish_window()
+
+    @pl.when(core == 0)
+    def _():
+        ordered_v[0:WIN, :] = win_weights[...]
+        for d in range(xs):
+            @pl.when(x == d)
+            def _():
+                b3c(d, False).start()
+                out_block(d).start()
+
     own_update()
     for out in outs[1:4]:
         out.start()
-    for d in sorted(range(1, xs), key=lambda d: min(d, xs - d)):
-        for far in range(2):
-            b3x(d, far, True).wait_recv()
-        finish_block(d)
     for d in range(xs):
         b3c(d, True).wait_recv()
 
@@ -687,7 +714,8 @@
     for i in range(xs):
         p1a(i).wait_send()
     for d in range(1, xs):
-        p1b(d).wait_send()
+        p1b(d, 0).wait_send()
+        p1b(d, 1).wait_send()
     for d in range(1, ys):
         p2(d).wait_send()
         wy(d, False).wait_send()
@@ -790,6 +818,7 @@
             pltpu.VMEM((3, shard_rows, LANES), f32),
             pltpu.VMEM((all_rows, LANES), bf16),
             pltpu.VMEM((all_rows, LANES), bf16),
+            pltpu.VMEM((16, LANES), bf16),
             pltpu.VMEM((all_rows, LANES), bf16),
             pltpu.VMEM((256, cells + 2 * LANES), bf16),
             pltpu.VMEM((8 * emb, cells), bf16),
@@ -825,7 +854,7 @@
             dma((16,)), dma((4 + ss,)),
             dma((2,)), dma((2,)), dma((2,)), dma((2,)),
             dma((ss // 2,)), dma((ss // 2,)),
-            dma((max(ss // 2 - 1, 1),)), dma((max(ss // 2 - 1, 1),)),
+            dma((max(ss // 2 - 1, 1), 2)), dma((max(ss // 2 - 1, 1), 2)),
             dma((ys - 1,)), dma((ys - 1,)),
             dma((zs - 1,)), dma((zs - 1,)),
             dma((zs - 1,)), dma,

time: 46 us -> 45.2 us (0.983)
  Pallas kernels: 45.2 us -> 44.5 us
    pallas_call x1, Pallas kernels: 43.2 us -> 42.4 us  [on_device(): pl.pallas_call(functools.partial(kernel, sizes), out_shape=(jax.ShapeDtyp...]
where the time goes in v5:
time: 45.2 us; the launch traced here: 45.1 us
  Pallas kernels  44.5 us (98%)
  between operations  0.64 us (1%)
    pallas_call x1, Pallas kernels, on_device(): pl.pallas_call(functools.partial(kernel, sizes), out_shape=(jax.ShapeDtyp...  42.4 us
    pallas_call x1, Pallas kernels, on_device(): pl.pallas_call(copy_kernel, out_shape=tuple((jax.ShapeDtypeStruct(out.sha...  2.05 us

profile of v5, /device:TPU:1, one launch (start us, length us, event | category | flops | bytes accessed | tf_op | source)
XLA Modules:
  0.0 45.1 jit_solution(12388547200960294050)
XLA Ops:
  0.6 42.4 %shard_map.191 = (bf16[24,4,8,128]{3,2,1,0:T(8,128)(2,1)}, f32[32,128]{1,0:T(8,128)}, f32[32,128]{1,0:T(8,128)}, f32[32,128]{1,0:T(8,128)}, bf16[2048,128]{1,0:T(8,128)(2,1)}) custom-call(bf16[24,4,8,128]{3,2,1,0:T(8,128)(2,1)} %bitcast.15, bf16[16,4,8,128]{3,2,1,0:T(8,128)(2,1)} %bitcast.17, bf16[27,24,24]{2,1,0:T(8,128)(2,1)} %bitcast.16, ...), custom_call_target="tpu_custom_call" | custom-call | tf_op jit(solution)/shard_map/pallas_call | solution.py:797
  43.1 2.0 %shard_map.192 = (bf16[24,4,8,128]{3,2,1,0:T(8,128)(2,1)}, f32[32,128]{1,0:T(8,128)}, f32[32,128]{1,0:T(8,128)}, f32[32,128]{1,0:T(8,128)}, bf16[2048,128]{1,0:T(8,128)(2,1)}) custom-call(bf16[24,4,8,128]{3,2,1,0:T(8,128)(2,1)} %get-tuple-element.15.refs_0_, f32[32,128]{1,0:T(8,128)} %get-tuple-element.16.refs_1_, f32[32,128]{1,0:T(8,128)} %get-tuple-element.17.refs_2_, ...), custom_call_target="tpu_custom_call" | custom-call | tf_op jit(solution)/shard_map/pallas_call | solution.py:887

commit v6 on v5

--- a/solution.py
+++ b/solution.py
@@ -220,9 +220,15 @@
     def block(ref, xx, cc):
         return ref.at[pl.ds(pl.multiple_of((xx * 2 + cc) * block_rows, 16), block_rows)]
 
-    def p1a(i):
+    def part_rows(part):
+        return (far_rows, block_rows - far_rows) if part else (0, far_rows)
+
+    def p1a(i, part):
+        start, count = part_rows(part)
+        at_row = (i * 2 + 1 - core) * block_rows + start
         return remote(
-            block(flat_b, i, 1 - core), p1a_recv.at[i], p1a_ssem.at[i], p1a_rsem.at[i], at(z, y, x * 2 + 1 - core)
+            flat_b.at[pl.ds(pl.multiple_of(at_row, 16), count)], p1a_recv.at[i, pl.ds(start, count)],
+            p1a_ssem.at[i, part], p1a_rsem.at[i, part], at(z, y, x * 2 + 1 - core),
         )
 
     def p1b(d, part):
@@ -234,8 +240,9 @@
         )
 
     order = [(x + d) % xs for d in far_first(xs) + [0]]
-    for i in order:
-        p1a(i).start()
+    for part in range(2):
+        for i in order:
+            p1a(i, part).start()
 
     copies[0].wait()
     for p in range(planes):
@@ -283,15 +290,17 @@
 
     start_halo(fh_send, fh_recv, fh_ssem, fh_rsem)
 
-    for d in far_first(xs) + [0]:
-        to = (x + d) % xs
-        p1a(to).wait_recv()
-        own = flat_b[pl.ds(pl.multiple_of((to * 2 + core) * block_rows, 16), block_rows), :].astype(f32)
-        pair_sum[to] = (own + p1a_recv[to].astype(f32)).astype(bf16)
-        if d:
-            p1b(d, 0).start()
-    for d in far_first(xs):
-        p1b(d, 1).start()
+    for part in range(2):
+        start, count = part_rows(part)
+        for d in far_first(xs) + [0]:
+            to = (x + d) % xs
+            p1a(to, part).wait_recv()
+            own_row = pl.multiple_of((to * 2 + core) * block_rows + start, 16)
+            own = flat_b[pl.ds(own_row, count), :].astype(f32)
+            total = own + p1a_recv[to, start : start + count].astype(f32)
+            pair_sum[to, start : start + count] = total.astype(bf16)
+            if d:
+                p1b(d, part).start()
 
     for i in (13, 14, 15):
         copies[i].wait()
@@ -712,7 +721,8 @@
         w1(d).wait_send()
         wb(d, False).wait_send()
     for i in range(xs):
-        p1a(i).wait_send()
+        p1a(i, 0).wait_send()
+        p1a(i, 1).wait_send()
     for d in range(1, xs):
         p1b(d, 0).wait_send()
         p1b(d, 1).wait_send()
@@ -853,7 +863,7 @@
             pltpu.VMEM((WIN, LANES), bf16),
             dma((16,)), dma((4 + ss,)),
             dma((2,)), dma((2,)), dma((2,)), dma((2,)),
-            dma((ss // 2,)), dma((ss // 2,)),
+            dma((ss // 2, 2)), dma((ss // 2, 2)),
             dma((max(ss // 2 - 1, 1), 2)), dma((max(ss // 2 - 1, 1), 2)),
             dma((ys - 1,)), dma((ys - 1,)),
             dma((zs - 1,)), dma((zs - 1,)),

time: 45.2 us -> 45.4 us (level)
  no operation moved by 1% of the time
where the time goes in v6:
time: 45.4 us; the launch traced here: 45.2 us
  Pallas kernels  44.6 us (98%)
  between operations  0.64 us (1%)
    pallas_call x1, Pallas kernels, on_device(): pl.pallas_call(functools.partial(kernel, sizes), out_shape=(jax.ShapeDtyp...  42.6 us
    pallas_call x1, Pallas kernels, on_device(): pl.pallas_call(copy_kernel, out_shape=tuple((jax.ShapeDtypeStruct(out.sha...  2.05 us

profile of v6, /device:TPU:1, one launch (start us, length us, event | category | flops | bytes accessed | tf_op | source)
XLA Modules:
  0.0 45.2 jit_solution(17538560110183533074)
XLA Ops:
  0.6 42.6 %shard_map.191 = (bf16[24,4,8,128]{3,2,1,0:T(8,128)(2,1)}, f32[32,128]{1,0:T(8,128)}, f32[32,128]{1,0:T(8,128)}, f32[32,128]{1,0:T(8,128)}, bf16[2048,128]{1,0:T(8,128)(2,1)}) custom-call(bf16[24,4,8,128]{3,2,1,0:T(8,128)(2,1)} %bitcast.15, bf16[16,4,8,128]{3,2,1,0:T(8,128)(2,1)} %bitcast.17, bf16[27,24,24]{2,1,0:T(8,128)(2,1)} %bitcast.16, ...), custom_call_target="tpu_custom_call" | custom-call | tf_op jit(solution)/shard_map/pallas_call | solution.py:807
  43.2 2.0 %shard_map.192 = (bf16[24,4,8,128]{3,2,1,0:T(8,128)(2,1)}, f32[32,128]{1,0:T(8,128)}, f32[32,128]{1,0:T(8,128)}, f32[32,128]{1,0:T(8,128)}, bf16[2048,128]{1,0:T(8,128)(2,1)}) custom-call(bf16[24,4,8,128]{3,2,1,0:T(8,128)(2,1)} %get-tuple-element.15.refs_0_, f32[32,128]{1,0:T(8,128)} %get-tuple-element.16.refs_1_, f32[32,128]{1,0:T(8,128)} %get-tuple-element.17.refs_2_, ...), custom_call_target="tpu_custom_call" | custom-call | tf_op jit(solution)/shard_map/pallas_call | solution.py:897
